TPU v7x, 512 devices: a whole 4x4x16 slice. The times are simulated.
512 devices in a mesh: prompt: 16 (over y_hi, x, core), resp: 32 (over y_lo, z).
Axes of the slice: x: 4, y: 4 (y_hi: 2, y_lo: 2; y = y_hi * 2 + y_lo), z: 16, core: 2. Of those that a mesh axis runs over, the one named last changes fastest.
Arguments:
- query_prompt: bfloat16 [16, 1024, 2048], P('prompt', 'resp'), may hold values from -5 to 5
- query_resp: bfloat16 [16, 4096, 2048], P('prompt', 'resp'), may hold values from -6 to 6
- kv_prompt: bfloat16 [16, 1024, 1024], P('prompt', 'resp'), may hold values from -5 to 5
- kv_resp: bfloat16 [16, 4096, 1024], P('prompt', 'resp'), may hold values from -6 to 6
- grad_prompt: bfloat16 [16, 1024, 2048], P('prompt', 'resp'), may hold values from -24 to 24
- grad_resp: bfloat16 [16, 4096, 2048], P('prompt', 'resp'), may hold values from -24 to 24
- norm_gains: float32 [2, 128], replicated, may hold values from 0.5 to 4.5
- resp_lengths: int32 [16, 17], P('prompt'), may hold values from 1 to 1024, 4096 in all within a row
Outputs:
- dq_prompt: bfloat16 [16, 1024, 2048], P('prompt', 'resp')
- dq_resp: bfloat16 [16, 4096, 2048], P('prompt', 'resp')
- dkv_prompt: bfloat16 [16, 1024, 1024], P('prompt', 'resp')
- dkv_resp: bfloat16 [16, 4096, 1024], P('prompt', 'resp')
- norm_grads: float32 [2, 128], replicated
Inputs may be any that keep to these rules, and one draw needn't show every extreme that they name: `resp_lengths`: each group's lengths sum to 4096; the largest is exactly 1024.
All inputs are finite; a program needn't handle non-finite values.
Results may differ from a plain program's by a relative error of at most 0.03.
The roundings to bfloat16 on the way count: a program that leaves them out, or rounds other values in their place, can miss the bound.
Values may be sent and summed in bfloat16 or wider, within the bound.
A program may use at most 128 MiB of HBM per device.

v0:
```python
import jax
import jax.numpy as jnp
from jax import lax
from jax.sharding import PartitionSpec as P

QHEADS = 16
KVHEADS = 4
HEADDIM = 128
SHARING = 4


epsilon = 1e-06


def from_behind(value, axis, steps):
    count = lax.axis_size(axis)
    leading, last = (max(0, -steps), min(count, count - steps))
    return lax.ppermute(value, axis, [(source, source + steps) for source in range(leading, last)])


def normalize(raw, gain, heads):
    values = raw.astype(jnp.float32).reshape(raw.shape[0], heads, HEADDIM)
    factor = lax.rsqrt(jnp.mean(values * values, axis=-1, keepdims=True) + epsilon)
    normed = values * factor
    return ((normed * gain).astype(jnp.bfloat16), normed, factor)


def norm_back(upstream, normed, factor, gain):
    scaled = upstream * gain
    inner = jnp.mean(scaled * normed, axis=-1, keepdims=True)
    return (factor * (scaled - normed * inner), jnp.sum(upstream * normed, axis=(0, 1)))


def segment_of(index, ends):
    return jnp.sum((index[:, None] >= ends[None, :]).astype(jnp.int32), axis=1)


def resp_mask(query_index, key_index, ends):
    same = segment_of(query_index, ends)[:, None] == segment_of(key_index, ends)[None, :]
    return (key_index[None, :] >= 0) & same & (key_index[None, :] <= query_index[:, None])


def head_back(queries, upstream, keys, values, allowed):
    scale = HEADDIM ** (-0.5)
    scores = jnp.einsum("rgd,kd->rgk", queries, keys, preferred_element_type=jnp.float32) * scale
    scores = jnp.where(allowed[:, None, :], scores, -jnp.inf)
    top = jnp.max(scores, axis=-1, keepdims=True)
    expo = jnp.exp(scores - top)
    probs = expo / jnp.sum(expo, axis=-1, keepdims=True)
    probs_low = probs.astype(jnp.bfloat16)
    output = jnp.einsum("rgk,kd->rgd", probs_low, values, preferred_element_type=jnp.float32)
    out_low = lax.optimization_barrier(output.astype(jnp.bfloat16))
    delta = jnp.sum(
        upstream.astype(jnp.float32) * out_low.astype(jnp.float32), axis=-1, keepdims=True
    )
    grad_values = jnp.einsum("rgk,rgd->kd", probs_low, upstream, preferred_element_type=jnp.float32)
    grad_probs = jnp.einsum("rgd,kd->rgk", upstream, values, preferred_element_type=jnp.float32)
    ds_low = (probs * (grad_probs - delta)).astype(jnp.bfloat16)
    grad_queries = scale * jnp.einsum(
        "rgk,kd->rgd", ds_low, keys, preferred_element_type=jnp.float32
    )
    grad_keys = scale * jnp.einsum(
        "rgk,rgd->kd", ds_low, queries, preferred_element_type=jnp.float32
    )
    return (grad_queries, grad_keys, grad_values)


def run_heads(queries, upstream, keys, values, allowed):

    def per_head(inputs):
        return head_back(inputs[0], inputs[1], inputs[2], inputs[3], allowed)

    return lax.map(per_head, (queries, upstream, keys, values))


def by_heads(rows, count):
    return rows.reshape(count, KVHEADS, SHARING, HEADDIM).transpose(1, 0, 2, 3)


def key_heads(rows, count):
    return rows.reshape(count, KVHEADS, HEADDIM).transpose(1, 0, 2)


def per_device(
    query_prompt, query_resp, kv_prompt, kv_resp, grad_prompt, grad_resp, norm_gains, resp_lengths
):
    width = KVHEADS * HEADDIM
    prompt_rows = query_prompt.shape[1]
    resp_rows = query_resp.shape[1]
    reach = lax.axis_size("resp") // 4
    device = lax.axis_index("resp")
    qn_p, qhat_p, qfac_p = normalize(query_prompt[0], norm_gains[0], QHEADS)
    qn_r, qhat_r, qfac_r = normalize(query_resp[0], norm_gains[0], QHEADS)
    kn_p, khat_p, kfac_p = normalize(kv_prompt[0][:, :width], norm_gains[1], KVHEADS)
    kn_r, khat_r, kfac_r = normalize(kv_resp[0][:, :width], norm_gains[1], KVHEADS)
    full_keys, full_vals = (
        lax.all_gather(kn_p.reshape(prompt_rows, width), "resp", axis=0, tiled=True),
        lax.all_gather(kv_prompt[0][:, width:], "resp", axis=0, tiled=True),
    )
    own_pair = jnp.stack([kn_r.reshape(resp_rows, width), kv_resp[0][:, width:]])
    earlier = [from_behind(own_pair, "resp", offset) for offset in range(1, reach + 1)]
    ordered = earlier[::-1] + [own_pair]
    total_prompt = full_keys.shape[0]
    all_keys = jnp.concatenate([full_keys] + [pair[0] for pair in ordered], axis=0)
    all_vals = jnp.concatenate([full_vals] + [pair[1] for pair in ordered], axis=0)
    key_count = all_keys.shape[0]
    window = (reach + 1) * resp_rows
    ends = jnp.cumsum(resp_lengths[0])
    prompt_query = device * prompt_rows + jnp.arange(prompt_rows, dtype=jnp.int32)
    prompt_key = jnp.arange(total_prompt, dtype=jnp.int32)
    resp_query = device * resp_rows + jnp.arange(resp_rows, dtype=jnp.int32)
    resp_key = (device - reach) * resp_rows + jnp.arange(window, dtype=jnp.int32)
    upper_mask = prompt_query[:, None] >= prompt_key[None, :]
    lower_mask = jnp.concatenate(
        [jnp.ones((resp_rows, total_prompt), bool), resp_mask(resp_query, resp_key, ends)], axis=1
    )
    gq_p, gk_p, gv_p = run_heads(
        by_heads(qn_p, prompt_rows),
        by_heads(grad_prompt[0], prompt_rows),
        key_heads(full_keys, total_prompt),
        key_heads(full_vals, total_prompt),
        upper_mask,
    )
    gq_r, gk_r, gv_r = run_heads(
        by_heads(qn_r, resp_rows),
        by_heads(grad_resp[0], resp_rows),
        key_heads(all_keys, key_count),
        key_heads(all_vals, key_count),
        lower_mask,
    )
    grad_q_p = gq_p.transpose(1, 0, 2, 3).reshape(prompt_rows, QHEADS, HEADDIM)
    grad_q_r = gq_r.transpose(1, 0, 2, 3).reshape(resp_rows, QHEADS, HEADDIM)
    grad_k = gk_r.transpose(1, 0, 2).reshape(key_count, width)
    grad_v = gv_r.transpose(1, 0, 2).reshape(key_count, width)
    prompt_k = gk_p.transpose(1, 0, 2).reshape(total_prompt, width) + grad_k[:total_prompt]
    prompt_v = gv_p.transpose(1, 0, 2).reshape(total_prompt, width) + grad_v[:total_prompt]
    summed_k, summed_v = (
        lax.psum(prompt_k.astype(jnp.bfloat16), "resp").astype(jnp.float32),
        lax.psum(prompt_v.astype(jnp.bfloat16), "resp").astype(jnp.float32),
    )
    mine_k = lax.dynamic_slice_in_dim(summed_k, device * prompt_rows, prompt_rows, 0)
    mine_v = lax.dynamic_slice_in_dim(summed_v, device * prompt_rows, prompt_rows, 0)

    def partial_rows(offset):
        start = total_prompt + (reach - offset) * resp_rows
        return jnp.stack([grad_k[start : start + resp_rows], grad_v[start : start + resp_rows]])

    returned = partial_rows(0)
    for offset in range(1, reach + 1):
        returned = returned + from_behind(
            partial_rows(offset).astype(jnp.bfloat16), "resp", -offset
        ).astype(jnp.float32)
    raw_qp, gain_qp = norm_back(grad_q_p, qhat_p, qfac_p, norm_gains[0])
    raw_qr, gain_qr = norm_back(grad_q_r, qhat_r, qfac_r, norm_gains[0])
    raw_kp, gain_kp = norm_back(
        mine_k.reshape(prompt_rows, KVHEADS, HEADDIM), khat_p, kfac_p, norm_gains[1]
    )
    raw_kr, gain_kr = norm_back(
        returned[0].reshape(resp_rows, KVHEADS, HEADDIM), khat_r, kfac_r, norm_gains[1]
    )
    gain_parts = jnp.stack([gain_qp + gain_qr, gain_kp + gain_kr])
    count = lax.axis_size("prompt") * (prompt_rows + resp_rows) * lax.axis_size("resp")
    scales = jnp.array([[(count * QHEADS) ** (-0.5)], [(count * KVHEADS) ** (-0.5)]], jnp.float32)
    norm_grads = lax.psum(gain_parts, ("prompt", "resp")) * scales
    out_qp = raw_qp.reshape(1, prompt_rows, QHEADS * HEADDIM).astype(jnp.bfloat16)
    out_qr = raw_qr.reshape(1, resp_rows, QHEADS * HEADDIM).astype(jnp.bfloat16)
    out_kp = jnp.concatenate([raw_kp.reshape(prompt_rows, width), mine_v], axis=1).astype(
        jnp.bfloat16
    )[None]
    out_kr = jnp.concatenate([raw_kr.reshape(resp_rows, width), returned[1]], axis=1).astype(
        jnp.bfloat16
    )[None]
    return (out_qp, out_qr, out_kp, out_kr, norm_grads)


def solution(mesh):
    return jax.shard_map(
        per_device,
        mesh=mesh,
        in_specs=(
            P("prompt", "resp", None),
            P("prompt", "resp", None),
            P("prompt", "resp", None),
            P("prompt", "resp", None),
            P("prompt", "resp", None),
            P("prompt", "resp", None),
            P(),
            P("prompt", None),
        ),
        out_specs=(
            P("prompt", "resp", None),
            P("prompt", "resp", None),
            P("prompt", "resp", None),
            P("prompt", "resp", None),
            P(),
        ),
        check_vma=False,
    )
```

profile of v0, /device:TPU:1, one launch (start us, length us, event | category | flops | bytes accessed | tf_op | source)
XLA Modules:
  0.0 999.2 jit_solution(5866174067182291449)
XLA Ops:
  14.9 17.0 %collective-permute-start = (bf16[2,128,512]{2,1,0:T(8,128)(2,1)}, bf16[2,128,512]{2,1,0:T(8,128)(2,1)}, u32[]{:S(2)}, u32[]{:S(2)}) collective-permute-start(bf16[2,128,512]{2,1,0:T(8,128)(2,1)} %pad_maximum_fusion), channel_id=1, source_target_pairs={{0,8},{1,9},{2,10},{3,11},{4,12},{5,13},{6,14},{7,15},{8,16},{9,17... | collective-permute-start | bytes 786440 | tf_op jit(solution)/shard_map/ppermute | solution.py:18
  31.8 6.1 collective-permute-start.1
  37.9 4.4 collective-permute-start.2
  42.3 8.4 collective-permute-start.3
  50.7 4.0 collective-permute-start.4
  69.7 30.9 %collective-permute-done.1 = bf16[2,128,512]{2,1,0:T(8,128)(2,1)} collective-permute-done((bf16[2,128,512]{2,1,0:T(8,128)(2,1)}, bf16[2,128,512]{2,1,0:T(8,128)(2,1)}, u32[]{:S(2)}, u32[]{:S(2)}) %collective-permute-start.1) | collective-permute-done | bytes 262176 | tf_op jit(solution)/shard_map/ppermute | solution.py:18
  102.9 4.9 collective-permute-done.2
  107.8 27.1 %collective-permute-start.7 = (bf16[2,128,512]{2,1,0:T(8,128)(2,1)}, bf16[2,128,512]{2,1,0:T(8,128)(2,1)S(1)}, u32[]{:S(2)}, u32[]{:S(2)}) collective-permute-start(bf16[2,128,512]{2,1,0:T(8,128)(2,1)} %pad_maximum_fusion), channel_id=1, source_target_pairs={{0,1},{1,2},{2,3},{3,4},{4,5},{5,6},{6,7},{7,8},{8,9},{9,10},{10,1... | collective-permute-start | bytes 786440 | tf_op jit(solution)/shard_map/ppermute | solution.py:18
  135.9 18.5 %collective-permute-done.3 = bf16[2,128,512]{2,1,0:T(8,128)(2,1)} collective-permute-done((bf16[2,128,512]{2,1,0:T(8,128)(2,1)}, bf16[2,128,512]{2,1,0:T(8,128)(2,1)}, u32[]{:S(2)}, u32[]{:S(2)}) %collective-permute-start.3) | collective-permute-done | bytes 262176 | tf_op jit(solution)/shard_map/ppermute | solution.py:18
  155.3 11.7 %collective-permute-done.4 = bf16[2,128,512]{2,1,0:T(8,128)(2,1)} collective-permute-done((bf16[2,128,512]{2,1,0:T(8,128)(2,1)}, bf16[2,128,512]{2,1,0:T(8,128)(2,1)}, u32[]{:S(2)}, u32[]{:S(2)}) %collective-permute-start.4) | collective-permute-done | bytes 262176 | tf_op jit(solution)/shard_map/ppermute | solution.py:18
  168.0 25.4 %collective-permute-done.5 = bf16[2,128,512]{2,1,0:T(8,128)(2,1)S(1)} collective-permute-done((bf16[2,128,512]{2,1,0:T(8,128)(2,1)}, bf16[2,128,512]{2,1,0:T(8,128)(2,1)S(1)}, u32[]{:S(2)}, u32[]{:S(2)}) %collective-permute-start.5) | collective-permute-done | bytes 262176 | tf_op jit(solution)/shard_map/ppermute | solution.py:18
  195.0 9.5 collective-permute-done.6
  205.3 10.9 %collective-permute-done.7 = bf16[2,128,512]{2,1,0:T(8,128)(2,1)S(1)} collective-permute-done((bf16[2,128,512]{2,1,0:T(8,128)(2,1)}, bf16[2,128,512]{2,1,0:T(8,128)(2,1)S(1)}, u32[]{:S(2)}, u32[]{:S(2)}) %collective-permute-start.7) | collective-permute-done | bytes 262176 | tf_op jit(solution)/shard_map/ppermute | solution.py:18
  222.4 38.4 %all-gather.3.cloned.1.call-done = bf16[1024,512]{1,0:T(8,128)(2,1)} async-done(((bf16[32,512]{1,0:T(8,128)(2,1)}), bf16[1024,512]{1,0:T(8,128)(2,1)}) %all-gather.3.cloned.1.call-update) | async-done | bytes 1048592 | tf_op jit(solution)/shard_map/all_gather | solution.py:97
  266.3 115.3 %all-gather.5.cloned.1.call-done = bf16[1024,512]{1,0:T(8,128)(2,1)} async-done(((bf16[32,512]{1,0:T(8,128)(2,1)}), bf16[1024,512]{1,0:T(8,128)(2,1)}) %all-gather.5.cloned.1.call-update) | async-done | bytes 1048592 | tf_op jit(solution)/shard_map/all_gather | solution.py:98
  388.4 83.2 %while.29 = (s32[]{:T(128)}, f32[4,128,4,128]{3,1,2,0:T(8,128)}, f32[4,2176,128]{2,1,0:T(8,128)}, f32[4,2176,128]{2,1,0:T(8,128)}, pred[128,2176]{1,0:T(8,128)(4...) while((s32[]{:T(128)}, f32[4,128,4,128]{3,1,2,0:T(8,128)}, ...), condition=%wide.region_17.18_spmd, body=%wide.region_13.17_spmd.sunk | while | flops 1723090560 | bytes 51019424 | solution.py:73
  388.4 5.3 fusion.216
  393.6 2.7 fusion.217
  398.5 3.5 fusion.218
  402.0 2.7 fusion.220
  406.5 2.7 fusion.219
  409.2 5.3 fusion.216
  414.4 2.7 fusion.217
  419.3 3.5 fusion.218
  422.8 2.7 fusion.220
  427.2 2.7 fusion.219
  429.9 5.3 fusion.216
  435.2 2.7 fusion.217
  440.0 3.5 fusion.218
  443.5 2.7 fusion.220
  448.0 2.7 fusion.219
  450.7 5.3 fusion.216
  455.9 2.7 fusion.217
  460.8 3.5 fusion.218
  464.3 2.7 fusion.220
  468.8 2.7 fusion.219
  471.5 4.3 bitcast_convert_fusion
  494.3 41.2 %while.30 = (s32[]{:T(128)}, f32[4,32,4,128]{3,1,2,0:T(8,128)}, f32[4,1024,128]{2,1,0:T(8,128)}, f32[4,1024,128]{2,1,0:T(8,128)}, bf16[4,32,4,128]{3,1,2,0:T(8,1...) while((s32[]{:T(128)}, f32[4,32,4,128]{3,1,2,0:T(8,128)}, ...), condition=%wide.region_6.7_spmd.clone, body=%wide.region_2.6_spmd.clone.sunk | while | flops 271060096 | bytes 5026537 | solution.py:73
  501.7 2.1 fusion.240
  522.3 2.1 fusion.240
  532.6 2.1 fusion.240
  535.6 3.9 fusion.114
  542.0 2.6 multiply_reduce_fusion.2
  551.5 2.4 multiply_convert_fusion
  565.9 10.2 %collective-permute-done.13 = bf16[2,128,512]{2,1,0:T(8,128)(2,1)S(1)} collective-permute-done((bf16[2,128,512]{2,1,0:T(8,128)(2,1)}, bf16[2,128,512]{2,1,0:T(8,128)(2,1)S(1)}, u32[]{:S(2)}, u32[]{:S(2)}) %collective-permute-start.13) | collective-permute-done | bytes 262176 | tf_op jit(solution)/shard_map/ppermute | solution.py:18
  576.1 20.0 %collective-permute-done.14 = bf16[2,128,512]{2,1,0:T(8,128)(2,1)S(1)} collective-permute-done((bf16[2,128,512]{2,1,0:T(8,128)(2,1)}, bf16[2,128,512]{2,1,0:T(8,128)(2,1)S(1)}, u32[]{:S(2)}, u32[]{:S(2)}) %collective-permute-start.14) | collective-permute-done | bytes 262176 | tf_op jit(solution)/shard_map/ppermute | solution.py:18
  599.4 266.6 %all-reduce.4.cloned.1.call-done = (bf16[1024,512]{1,0:T(8,128)(2,1)}, bf16[1024,512]{1,0:T(8,128)(2,1)}) async-done(((bf16[1024,512]{1,0:T(8,128)(2,1)}, bf16[1024,512]{1,0:T(8,128)(2,1)}), (bf16[1024,512]{1,0:T(8,128)(2,1)}, bf16[1024,512]{1,0:T(8,128)(2,1)})) %all-reduce.4.cloned.1.call-update) | async-done | bytes 2097168 | tf_op jit(solution)/shard_map/psum | solution.py:139
  868.0 122.6 %psum.23 = f32[2,128]{1,0:T(2,128)S(1)} all-reduce(f32[2,128]{1,0:T(2,128)S(1)} %pad_maximum_fusion.11), channel_id=1, replica_groups=mesh['prompt'=16,'resp'=32] {'prompt','resp'}, use_global_device_ids=true, to_apply=%region_29.30 | all-reduce | flops 256 | bytes 2048 | tf_op jit(solution)/shard_map/psum | solution.py:164
  (393 shorter events, 144.9 us)
Async XLA Ops:
  7.2 47.7 %copy-start.5 = (bf16[1,128,2048]{2,1,0:T(8,128)(2,1)S(1)}, bf16[1,128,2048]{2,1,0:T(8,128)(2,1)}, u32[]{:S(2)}) copy-start(bf16[1,128,2048]{2,1,0:T(8,128)(2,1)} %param.14) | copy-start | bytes 1572868
  7.2 253.6 %all-gather.3.cloned.1.call-start = ((), (), s32[]{:S(2)}) async-start(), calls=%async_computation | async-start | bytes 1081344 | tf_op jit(solution)/shard_map/all_gather | solution.py:97
  8.0 46.8 %copy-start.53 = (f32[128]{0:T(128)}, f32[128]{0:T(128)S(1)}, u32[]{:S(2)}) copy-start(f32[128]{0:T(128)S(1)} %get-tuple-element.289) | copy-start | bytes 1540
  8.0 54.0 %copy-start.51 = (f32[128]{0:T(128)}, f32[128]{0:T(128)S(1)}, u32[]{:S(2)}) copy-start(f32[128]{0:T(128)S(1)} %get-tuple-element.290) | copy-start | bytes 1540
  8.0 46.8 %copy-start.48 = (f32[512]{0:T(512)}, f32[512]{0:T(512)S(1)}, u32[]{:S(2)}) copy-start(f32[512]{0:T(512)S(1)} %broadcast_bitcast_fusion.1) | copy-start | bytes 6148
  11.1 370.5 %all-gather.5.cloned.1.call-start = ((), (), s32[]{:S(2)}) async-start(), calls=%async_computation.1 | async-start | bytes 1081344 | tf_op jit(solution)/shard_map/all_gather | solution.py:98
  12.9 41.9 %copy-start.13 = (f32[128,4,128]{2,1,0:T(4,128)}, f32[128,4,128]{2,1,0:T(4,128)S(1)}, u32[]{:S(2)}) copy-start(f32[128,4,128]{2,1,0:T(4,128)S(1)} %reshape.504) | copy-start | bytes 786436
  13.2 41.7 %copy-start.22 = (f32[128,4]{1,0:T(8,128)}, f32[128,4]{1,0:T(8,128)S(1)}, u32[]{:S(2)}) copy-start(f32[128,4]{1,0:T(8,128)S(1)} %add_rsqrt_fusion) | copy-start | bytes 6148
  13.2 42.6 %copy-start.19 = (bf16[1,32,2048]{2,1,0:T(8,128)(2,1)S(1)}, bf16[1,32,2048]{2,1,0:T(8,128)(2,1)}, u32[]{:S(2)}) copy-start(bf16[1,32,2048]{2,1,0:T(8,128)(2,1)} %param.13) | copy-start | bytes 393220
  14.1 42.0 %copy-start.55 = (s32[1,17]{1,0:T(1,128)S(1)}, s32[1,17]{1,0:T(1,128)}, u32[]{:S(2)}) copy-start(s32[1,17]{1,0:T(1,128)} %param.20) | copy-start | bytes 208
  14.9 52.5 %collective-permute-start = (bf16[2,128,512]{2,1,0:T(8,128)(2,1)}, bf16[2,128,512]{2,1,0:T(8,128)(2,1)}, u32[]{:S(2)}, u32[]{:S(2)}) collective-permute-start(bf16[2,128,512]{2,1,0:T(8,128)(2,1)} %pad_maximum_fusion), channel_id=1, source_target_pairs={{0,8},{1,9},{2,10},{3,11},{4,12},{5,13},{6,14},{7,15},{8,16},{9,17... | collective-permute-start | bytes 786440 | tf_op jit(solution)/shard_map/ppermute | solution.py:18
  31.8 68.8 %collective-permute-start.1 = (bf16[2,128,512]{2,1,0:T(8,128)(2,1)}, bf16[2,128,512]{2,1,0:T(8,128)(2,1)}, u32[]{:S(2)}, u32[]{:S(2)}) collective-permute-start(bf16[2,128,512]{2,1,0:T(8,128)(2,1)} %pad_maximum_fusion), channel_id=1, source_target_pairs={{0,7},{1,8},{2,9},{3,10},{4,11},{5,12},{6,13},{7,14},{8,15},{9,16}... | collective-permute-start | bytes 786440 | tf_op jit(solution)/shard_map/ppermute | solution.py:18
  37.9 69.9 %collective-permute-start.2 = (bf16[2,128,512]{2,1,0:T(8,128)(2,1)}, bf16[2,128,512]{2,1,0:T(8,128)(2,1)}, u32[]{:S(2)}, u32[]{:S(2)}) collective-permute-start(bf16[2,128,512]{2,1,0:T(8,128)(2,1)} %pad_maximum_fusion), channel_id=1, source_target_pairs={{0,6},{1,7},{2,8},{3,9},{4,10},{5,11},{6,12},{7,13},{8,14},{9,15},... | collective-permute-start | bytes 786440 | tf_op jit(solution)/shard_map/ppermute | solution.py:18
  42.3 112.0 %collective-permute-start.3 = (bf16[2,128,512]{2,1,0:T(8,128)(2,1)}, bf16[2,128,512]{2,1,0:T(8,128)(2,1)}, u32[]{:S(2)}, u32[]{:S(2)}) collective-permute-start(bf16[2,128,512]{2,1,0:T(8,128)(2,1)} %pad_maximum_fusion), channel_id=1, source_target_pairs={{0,5},{1,6},{2,7},{3,8},{4,9},{5,10},{6,11},{7,12},{8,13},{9,14},{... | collective-permute-start | bytes 786440 | tf_op jit(solution)/shard_map/ppermute | solution.py:18
  50.7 116.4 %collective-permute-start.4 = (bf16[2,128,512]{2,1,0:T(8,128)(2,1)}, bf16[2,128,512]{2,1,0:T(8,128)(2,1)}, u32[]{:S(2)}, u32[]{:S(2)}) collective-permute-start(bf16[2,128,512]{2,1,0:T(8,128)(2,1)} %pad_maximum_fusion), channel_id=1, source_target_pairs={{0,4},{1,5},{2,6},{3,7},{4,8},{5,9},{6,10},{7,11},{8,12},{9,13},{1... | collective-permute-start | bytes 786440 | tf_op jit(solution)/shard_map/ppermute | solution.py:18
  54.7 811.3 %all-reduce.4.cloned.1.call-start = ((), (), s32[]{:S(2)}) async-start(), calls=%async_computation.2 | async-start | bytes 4194304 | tf_op jit(solution)/shard_map/psum | solution.py:139
  67.4 126.1 %collective-permute-start.5 = (bf16[2,128,512]{2,1,0:T(8,128)(2,1)}, bf16[2,128,512]{2,1,0:T(8,128)(2,1)S(1)}, u32[]{:S(2)}, u32[]{:S(2)}) collective-permute-start(bf16[2,128,512]{2,1,0:T(8,128)(2,1)} %pad_maximum_fusion), channel_id=1, source_target_pairs={{0,3},{1,4},{2,5},{3,6},{4,7},{5,8},{6,9},{7,10},{8,11},{9,12},{10... | collective-permute-start | bytes 786440 | tf_op jit(solution)/shard_map/ppermute | solution.py:18
  100.6 103.9 %collective-permute-start.6 = (bf16[2,128,512]{2,1,0:T(8,128)(2,1)}, bf16[2,128,512]{2,1,0:T(8,128)(2,1)S(1)}, u32[]{:S(2)}, u32[]{:S(2)}) collective-permute-start(bf16[2,128,512]{2,1,0:T(8,128)(2,1)} %pad_maximum_fusion), channel_id=1, source_target_pairs={{0,2},{1,3},{2,4},{3,5},{4,6},{5,7},{6,8},{7,9},{8,10},{9,11},{10,... | collective-permute-start | bytes 786440 | tf_op jit(solution)/shard_map/ppermute | solution.py:18
  107.8 108.4 %collective-permute-start.7 = (bf16[2,128,512]{2,1,0:T(8,128)(2,1)}, bf16[2,128,512]{2,1,0:T(8,128)(2,1)S(1)}, u32[]{:S(2)}, u32[]{:S(2)}) collective-permute-start(bf16[2,128,512]{2,1,0:T(8,128)(2,1)} %pad_maximum_fusion), channel_id=1, source_target_pairs={{0,1},{1,2},{2,3},{3,4},{4,5},{5,6},{6,7},{7,8},{8,9},{9,10},{10,1... | collective-permute-start | bytes 786440 | tf_op jit(solution)/shard_map/ppermute | solution.py:18
  264.1 120.7 %copy-start.34 = (bf16[128,4,128]{2,1,0:T(4,128)(2,1)S(1)}, bf16[128,4,128]{2,1,0:T(4,128)(2,1)}, u32[]{:S(2)}) copy-start(bf16[128,4,128]{2,1,0:T(4,128)(2,1)} %concatenate.88) | copy-start | bytes 393220
  264.2 120.7 %copy-start.35 = (bf16[128,4,128]{2,1,0:T(4,128)(2,1)S(1)}, bf16[128,4,128]{2,1,0:T(4,128)(2,1)}, u32[]{:S(2)}) copy-start(bf16[128,4,128]{2,1,0:T(4,128)(2,1)} %concatenate.89) | copy-start | bytes 393220
  264.2 120.7 %copy-start.36 = (bf16[128,4,128]{2,1,0:T(4,128)(2,1)S(1)}, bf16[128,4,128]{2,1,0:T(4,128)(2,1)}, u32[]{:S(2)}) copy-start(bf16[128,4,128]{2,1,0:T(4,128)(2,1)} %concatenate.90) | copy-start | bytes 393220
  264.3 120.7 %copy-start.37 = (bf16[128,4,128]{2,1,0:T(4,128)(2,1)S(1)}, bf16[128,4,128]{2,1,0:T(4,128)(2,1)}, u32[]{:S(2)}) copy-start(bf16[128,4,128]{2,1,0:T(4,128)(2,1)} %concatenate.91) | copy-start | bytes 393220
  266.3 120.7 %copy-start.38 = (bf16[16,4,8,128]{3,2,1,0:T(8,128)(2,1)S(1)}, bf16[16,4,8,128]{3,2,1,0:T(8,128)(2,1)}, u32[]{:S(2)}) copy-start(bf16[16,4,8,128]{3,2,1,0:T(8,128)(2,1)} %get-tuple-element.268) | copy-start | bytes 393220
  480.1 78.4 %collective-permute-start.8 = (bf16[2,128,512]{2,1,0:T(8,128)(2,1)}, bf16[2,128,512]{2,1,0:T(8,128)(2,1)}, u32[]{:S(2)}, u32[]{:S(2)}) collective-permute-start(bf16[2,128,512]{2,1,0:T(8,128)(2,1)} %pad_maximum_fusion.1), channel_id=1, source_target_pairs={{1,0},{2,1},{3,2},{4,3},{5,4},{6,5},{7,6},{8,7},{9,8},{10,9},{11,1... | collective-permute-start | bytes 786440 | tf_op jit(solution)/shard_map/ppermute | solution.py:18
  482.5 77.4 %collective-permute-start.9 = (bf16[2,128,512]{2,1,0:T(8,128)(2,1)}, bf16[2,128,512]{2,1,0:T(8,128)(2,1)}, u32[]{:S(2)}, u32[]{:S(2)}) collective-permute-start(bf16[2,128,512]{2,1,0:T(8,128)(2,1)} %pad_maximum_fusion.2), channel_id=1, source_target_pairs={{2,0},{3,1},{4,2},{5,3},{6,4},{7,5},{8,6},{9,7},{10,8},{11,9},{12,... | collective-permute-start | bytes 786440 | tf_op jit(solution)/shard_map/ppermute | solution.py:18
  483.9 7.4 copy-start.30
  484.1 8.0 copy-start.31
  484.9 8.0 copy-start.7
  484.9 76.3 %collective-permute-start.10 = (bf16[2,128,512]{2,1,0:T(8,128)(2,1)}, bf16[2,128,512]{2,1,0:T(8,128)(2,1)}, u32[]{:S(2)}, u32[]{:S(2)}) collective-permute-start(bf16[2,128,512]{2,1,0:T(8,128)(2,1)} %pad_maximum_fusion.3), channel_id=1, source_target_pairs={{3,0},{4,1},{5,2},{6,3},{7,4},{8,5},{9,6},{10,7},{11,8},{12,9},{13... | collective-permute-start | bytes 786440 | tf_op jit(solution)/shard_map/ppermute | solution.py:18
  487.4 78.5 %collective-permute-start.11 = (bf16[2,128,512]{2,1,0:T(8,128)(2,1)}, bf16[2,128,512]{2,1,0:T(8,128)(2,1)}, u32[]{:S(2)}, u32[]{:S(2)}) collective-permute-start(bf16[2,128,512]{2,1,0:T(8,128)(2,1)} %pad_maximum_fusion.4), channel_id=1, source_target_pairs={{4,0},{5,1},{6,2},{7,3},{8,4},{9,5},{10,6},{11,7},{12,8},{13,9},{1... | collective-permute-start | bytes 786440 | tf_op jit(solution)/shard_map/ppermute | solution.py:18
  489.7 76.1 %collective-permute-start.12 = (bf16[2,128,512]{2,1,0:T(8,128)(2,1)}, bf16[2,128,512]{2,1,0:T(8,128)(2,1)}, u32[]{:S(2)}, u32[]{:S(2)}) collective-permute-start(bf16[2,128,512]{2,1,0:T(8,128)(2,1)} %pad_maximum_fusion.5), channel_id=1, source_target_pairs={{5,0},{6,1},{7,2},{8,3},{9,4},{10,5},{11,6},{12,7},{13,8},{14,9},{... | collective-permute-start | bytes 786440 | tf_op jit(solution)/shard_map/ppermute | solution.py:18
  554.8 7.7 copy-start.21
  554.8 7.7 copy-start.45
  558.5 7.3 copy-start.57
  558.6 17.5 %collective-permute-start.13 = (bf16[2,128,512]{2,1,0:T(8,128)(2,1)}, bf16[2,128,512]{2,1,0:T(8,128)(2,1)S(1)}, u32[]{:S(2)}, u32[]{:S(2)}) collective-permute-start(bf16[2,128,512]{2,1,0:T(8,128)(2,1)} %pad_maximum_fusion.6), channel_id=1, source_target_pairs={{6,0},{7,1},{8,2},{9,3},{10,4},{11,5},{12,6},{13,7},{14,8},{15,9},... | collective-permute-start | bytes 786440 | tf_op jit(solution)/shard_map/ppermute | solution.py:18
  559.9 36.2 %collective-permute-start.14 = (bf16[2,128,512]{2,1,0:T(8,128)(2,1)}, bf16[2,128,512]{2,1,0:T(8,128)(2,1)S(1)}, u32[]{:S(2)}, u32[]{:S(2)}) collective-permute-start(bf16[2,128,512]{2,1,0:T(8,128)(2,1)} %pad_maximum_fusion.7), channel_id=1, source_target_pairs={{7,0},{8,1},{9,2},{10,3},{11,4},{12,5},{13,6},{14,7},{15,8},{16,9}... | collective-permute-start | bytes 786440 | tf_op jit(solution)/shard_map/ppermute | solution.py:18
  561.2 34.9 %collective-permute-start.15 = (bf16[2,128,512]{2,1,0:T(8,128)(2,1)S(1)}, bf16[2,128,512]{2,1,0:T(8,128)(2,1)S(1)}, u32[]{:S(2)}, u32[]{:S(2)}) collective-permute-start(bf16[2,128,512]{2,1,0:T(8,128)(2,1)S(1)} %pad_maximum_fusion.8), channel_id=1, source_target_pairs={{8,0},{9,1},{10,2},{11,3},{12,4},{13,5},{14,6},{15,7},{16,8},{17,9... | collective-permute-start | bytes 786440 | tf_op jit(solution)/shard_map/ppermute | solution.py:18
  565.5 32.2 %copy-start.10 = (f32[128,4,128]{2,1,0:T(4,128)S(1)}, f32[128,4,128]{2,1,0:T(4,128)}, u32[]{:S(2)}) copy-start(f32[128,4,128]{2,1,0:T(4,128)} %copy-done.9) | copy-start | bytes 786436
  565.5 32.2 %copy-start.18 = (bf16[1,128,1024]{2,1,0:T(8,128)(2,1)S(1)}, bf16[1,128,1024]{2,1,0:T(8,128)(2,1)}, u32[]{:S(2)}) copy-start(bf16[1,128,1024]{2,1,0:T(8,128)(2,1)} %param.16) | copy-start | bytes 786436
  565.8 32.2 %copy-start.14 = (f32[128,4,128]{2,1,0:T(4,128)S(1)}, f32[128,4,128]{2,1,0:T(4,128)}, u32[]{:S(2)}) copy-start(f32[128,4,128]{2,1,0:T(4,128)} %copy-done.13) | copy-start | bytes 786436
  565.8 32.1 %copy-start.23 = (f32[128,4]{1,0:T(8,128)S(1)}, f32[128,4]{1,0:T(8,128)}, u32[]{:S(2)}) copy-start(f32[128,4]{1,0:T(8,128)} %copy-done.22) | copy-start | bytes 6148
  565.8 32.1 %copy-start.54 = (f32[128]{0:T(128)S(1)}, f32[128]{0:T(128)}, u32[]{:S(2)}) copy-start(f32[128]{0:T(128)} %copy-done.53) | copy-start | bytes 1540
  565.8 32.7 %copy-start.49 = (f32[512]{0:T(512)S(1)}, f32[512]{0:T(512)}, u32[]{:S(2)}) copy-start(f32[512]{0:T(512)} %copy-done.48) | copy-start | bytes 6148
  597.7 269.1 %copy-start.27 = (f32[32,4,128]{2,1,0:T(4,128)S(1)}, f32[32,4,128]{2,1,0:T(4,128)}, u32[]{:S(2)}) copy-start(f32[32,4,128]{2,1,0:T(4,128)} %copy-done.26) | copy-start | bytes 196612
  597.7 269.4 %copy-start.25 = (f32[32,4,128]{2,1,0:T(4,128)S(1)}, f32[32,4,128]{2,1,0:T(4,128)}, u32[]{:S(2)}) copy-start(f32[32,4,128]{2,1,0:T(4,128)} %copy-done.24) | copy-start | bytes 196612
  597.7 269.4 %copy-start.41 = (bf16[1,32,1024]{2,1,0:T(8,128)(2,1)S(1)}, bf16[1,32,1024]{2,1,0:T(8,128)(2,1)}, u32[]{:S(2)}) copy-start(bf16[1,32,1024]{2,1,0:T(8,128)(2,1)} %param.15) | copy-start | bytes 196612
  597.8 393.5 %copy-start.56 = (f32[2]{0:T(128)S(1)}, f32[2]{0:T(128)}, u32[]{:S(2)}) copy-start(f32[2]{0:T(128)} %constant.105) | copy-start | bytes 28
  (36 other events, 133.3 us)
Sparse Core Ops, SparseCore 0:
  11.2 249.5 all-gather.2
  262.9 118.6 all-gather.4
  551.0 314.9 all-reduce.3
where the time goes:
time: 1000 us; the launch traced here: 999 us
  waiting for transfers between devices  562 us (56%)
  blocking collectives  123 us (12%)
  matrix products  106 us (11%)
  starting transfers between devices  80.2 us (8%)
  local copies, waits for them, and re-layouts  59.5 us (6%)
  other arithmetic  53.4 us (5%)
  between operations  15.1 us (2%)
    psum x1, waiting for transfers between devices, per_device(): lax.psum(prompt_v.astype(jnp.bfloat16), 'resp').astype(jnp.float32)  267 us
    ppermute x16, waiting for transfers between devices, from_behind(): lax.ppermute(value, axis, [(source, source + steps) for source in range(l...  142 us
    psum x1, blocking collectives, per_device(): norm_grads = lax.psum(gain_parts, ('prompt', 'resp')) * scales  123 us
    all_gather x1, waiting for transfers between devices, per_device(): lax.all_gather(kv_prompt[0][:, width:], 'resp', axis=0, tiled=True)  115 us
    ppermute x16, starting transfers between devices, from_behind(): lax.ppermute(value, axis, [(source, source + steps) for source in range(l...  80.1 us
    all_gather x1, waiting for transfers between devices, per_device(): lax.all_gather(kn_p.reshape(prompt_rows, width), 'resp', axis=0, tiled=True)  38.4 us
    sub x8, matrix products, head_back(): expo = jnp.exp(scores - top)  25.8 us
  transfers between devices with their start and end apart: 19, of which 12 were waited for; matrix products, arithmetic and copies ran while one was open for 11% of the time, Pallas kernels for 0%

commit v1 on v0

v1 whole, which is shorter than its diff:
```python
import functools

import jax
import jax.numpy as jnp
from jax import lax
from jax.experimental import pallas as pl
from jax.experimental.pallas import tpu as pltpu
from jax.sharding import PartitionSpec as P

MESH = pl.DeviceIdType.MESH
KH = 4
SH = 4
HD = 128
EPS = 1e-06
SCALE = HD ** (-0.5)
LOG2E = 1.4426950408889634
RROWS = 128
PROWS = 32
REACH = 8
NZ = 16
RC = SH * RROWS
PC = SH * PROWS
COLS = RC + PC
MASKED = -1e30
BF = jnp.bfloat16
F32 = jnp.float32


def dot(a, b):
    return lax.dot_general(a, b, (((1,), (0,)), ((), ())), preferred_element_type=F32)


def rms(x):
    factor = lax.rsqrt(jnp.mean(x * x, axis=-1, keepdims=True) + EPS)
    return x * factor, factor


def flip(index, bit):
    return index + (1 - 2 * ((index // bit) % 2)) * bit


def kernel(
    bits,
    total_rows,
    qp, qr, kvp, kvr, gp, gr, gains, lens,
    dqp, dqr, dkvp, dkvr, ngrad,
    win, pg, retr, rets, zr, zs, yr, ys, fin,
    qn, qt, do, dt, dqt, ew, dw, ep, dp,
    mref, lref, aref, mw, mp, red, redr,
    fs, fr, bs, br, azs, azr, ays, ayr, rzs, rzr, rys, ryr, rds, rdr,
):
    me = lax.axis_index("resp")
    pr = lax.axis_index("prompt")
    y = me // NZ
    z = me % NZ
    nxt = (me + 1) % (2 * NZ)
    prv = (me + 2 * NZ - 1) % (2 * NZ)
    znx = y * NZ + (z + 1) % NZ
    zpv = y * NZ + (z + NZ - 1) % NZ
    yp = (me + NZ) % (2 * NZ)

    partners = []
    for axis, bit in bits:
        if axis == "resp":
            partners.append((pr, flip(me, bit)))
        else:
            partners.append((flip(pr, bit), me))
    friends = [(pr, nxt), (pr, prv), (pr, znx), (pr, zpv), (pr, yp)] + partners

    barrier = pltpu.get_barrier_semaphore()
    for friend in friends:
        pl.semaphore_signal(barrier, inc=1, device_id=friend, device_id_type=MESH)

    g0 = gains[0:1, :]
    g1 = gains[1:2, :]

    def remote(src, dst, ssem, rsem, resp):
        return pltpu.make_async_remote_copy(
            src_ref=src, dst_ref=dst, send_sem=ssem, recv_sem=rsem,
            device_id=(pr, resp), device_id_type=MESH,
        )

    def fwd(k, h):
        return remote(win.at[k, h], win.at[k + 1, h], fs.at[k, h], fr.at[k, h], nxt)

    def back(k, h):
        return remote(rets.at[k - 1, h], retr.at[k - 1, h], bs.at[k - 1, h], br.at[k - 1, h], prv)

    def gather_z(t):
        return remote(pg.at[t, 0], pg.at[t + 1, 0], azs.at[t], azr.at[t], zpv)

    def gather_y(t):
        return remote(pg.at[t, 0], pg.at[t, 1], ays.at[t], ayr.at[t], yp)

    def scatter_z(t):
        return remote(zs.at[t - 1], zr.at[t - 1], rzs.at[t - 1], rzr.at[t - 1], znx)

    def scatter_y(t):
        return remote(ys.at[t], yr.at[t], rys.at[t], ryr.at[t], yp)

    for h in range(KH):
        cols = slice(h * HD, (h + 1) * HD)
        vcols = slice((KH + h) * HD, (KH + h + 1) * HD)
        khat, _ = rms(kvr[:, cols].astype(F32))
        win[0, h, :, 0:HD] = (khat * g1).astype(BF)
        win[0, h, :, HD : 2 * HD] = kvr[:, vcols]
        khat, _ = rms(kvp[:, cols].astype(F32))
        pg[0, 0, h, :, 0:HD] = (khat * g1).astype(BF)
        pg[0, 0, h, :, HD : 2 * HD] = kvp[:, vcols]

    pl.semaphore_wait(barrier, len(friends))
    gather_z(0).start()
    gather_y(0).start()
    for h in range(KH):
        fwd(0, h).start()

    for h in range(KH):
        for g in range(SH):
            head = h * SH + g
            cols = slice(head * HD, (head + 1) * HD)
            rows = slice(g * RROWS, (g + 1) * RROWS)
            prows = slice(RC + g * PROWS, RC + (g + 1) * PROWS)
            qhat, _ = rms(qr[:, cols].astype(F32))
            low = (qhat * g0).astype(BF)
            qn[h, rows, :] = low
            qt[h, :, rows] = low.astype(F32).T.astype(BF)
            qhat, _ = rms(qp[:, cols].astype(F32))
            qn[h, prows, :] = (qhat * g0).astype(BF)
            do[h, rows, :] = gr[:, cols]
            dt[h, :, rows] = gr[:, cols].astype(F32).T.astype(BF)
            do[h, prows, :] = gp[:, cols]
        qt[h, :, RC:COLS] = qn[h, RC:COLS, :].astype(F32).T.astype(BF)
        dt[h, :, RC:COLS] = do[h, RC:COLS, :].astype(F32).T.astype(BF)
        dqt[h] = jnp.zeros((HD, COLS), F32)

    lane = lax.broadcasted_iota(jnp.int32, (1, RC), 1)
    row_index = me * RROWS + lane % RROWS
    first = jnp.zeros((1, RC), jnp.int32)
    end = jnp.int32(0)
    for j in range(lens.shape[1]):
        end = end + lens[0, j]
        first = jnp.where(row_index >= end, end, first)

    def online(keys, vals, h, lo, hi, allowed, eref, dref, mold, lold, aold):
        cols = slice(lo, hi)
        scores = dot(keys, qt[h, :, cols]) * (SCALE * LOG2E)
        probs_grad = dot(vals, dt[h, :, cols])
        if allowed is not None:
            scores = jnp.where(allowed, scores, MASKED)
        top = jnp.maximum(mold, jnp.max(scores, axis=0, keepdims=True))
        shrink = jnp.exp2(mold - top)
        expo = jnp.exp2(scores - top)
        mref[h, :, cols] = top
        lref[h, :, cols] = lold * shrink + jnp.sum(expo, axis=0, keepdims=True)
        aref[h, :, cols] = aold * shrink + jnp.sum(expo * probs_grad, axis=0, keepdims=True)
        eref[:, cols] = expo
        dref[:, cols] = probs_grad
        return top

    def old(h, lo, hi):
        return mref[h, :, lo:hi], lref[h, :, lo:hi], aref[h, :, lo:hi]

    def key_rows(k):
        return (me - k) * RROWS + lax.broadcasted_iota(jnp.int32, (RROWS, RC), 0)

    def window_keys(k, h):
        return win[k, h, :, 0:HD], win[k, h, :, HD : 2 * HD]

    def forward_own(h):
        keys, vals = window_keys(0, h)
        index = key_rows(0)
        allowed = (index >= first) & (index <= row_index)
        start = jnp.full((1, RC), MASKED, F32)
        zero = jnp.zeros((1, RC), F32)
        top = online(keys, vals, h, 0, RC, allowed, ew.at[0, h], dw.at[0, h], start, zero, zero)
        mw[0, h] = top
        mref[h, :, RC:COLS] = jnp.full((1, PC), MASKED, F32)
        lref[h, :, RC:COLS] = jnp.zeros((1, PC), F32)
        aref[h, :, RC:COLS] = jnp.zeros((1, PC), F32)

    def forward_window(k, h):
        keys, vals = window_keys(k, h)
        allowed = key_rows(k) >= first
        mw[k, h] = online(keys, vals, h, 0, RC, allowed, ew.at[k, h], dw.at[k, h], *old(h, 0, RC))

    def prompt_keys(j, h):
        keys = pg[pl.ds(2 * j, 2), :, h, :, 0:HD].reshape(4 * PROWS, HD)
        vals = pg[pl.ds(2 * j, 2), :, h, :, HD : 2 * HD].reshape(4 * PROWS, HD)
        return keys, vals

    def forward_prompt(j, h):
        keys, vals = prompt_keys(j, h)
        sub = lax.broadcasted_iota(jnp.int32, (4 * PROWS, PC), 0)
        ring = jnp.where((sub & 32) == 0, y, 1 - y)
        chip = (z + 2 * j + (sub >> 6)) & (NZ - 1)
        position = (ring * NZ + chip) * PROWS + (sub & 31)
        query = me * PROWS + (lax.broadcasted_iota(jnp.int32, (4 * PROWS, PC), 1) & 31)
        er, dr = ep.at[j, h], dp.at[j, h]
        mp[j, h, :, 0:RC] = online(keys, vals, h, 0, RC, None, er, dr, *old(h, 0, RC))
        mp[j, h, :, RC:COLS] = online(
            keys, vals, h, RC, COLS, position <= query, er, dr, *old(h, RC, COLS)
        )

    def loop(count, body):
        def step(i, carry):
            body(i)
            return carry

        lax.fori_loop(0, count, step, 0)

    loop(KH, forward_own)

    def forward_step(n):
        k = n // KH
        h = n % KH
        fwd(k, h).wait_recv()

        @pl.when(k < REACH - 1)
        def _():
            fwd(k + 1, h).start()

        t = 2 * k + 1 + h // 2

        @pl.when((h % 2 == 0) & (t < NZ))
        def _():
            gather_z(t - 1).wait_recv()
            gather_y(t).start()

            @pl.when(t < NZ - 1)
            def _():
                gather_z(t).start()

        forward_window(k + 1, h)

        @pl.when(k >= 1)
        def _():
            @pl.when(h == 0)
            def _():
                gather_y(2 * k - 2).wait_recv()
                gather_y(2 * k - 1).wait_recv()

            forward_prompt(k - 1, h)

    loop(KH * REACH, forward_step)
    gather_y(NZ - 2).wait_recv()
    gather_y(NZ - 1).wait_recv()
    loop(KH, lambda h: forward_prompt(NZ // 2 - 1, h))

    def finish(h):
        inverse = 1.0 / lref[h]
        lref[h] = inverse
        aref[h] = aref[h] * inverse

    loop(KH, finish)

    def backward(keys, h, hi, top, eref, dref):
        weight = jnp.exp2(top - mref[h, :, 0:hi]) * lref[h, :, 0:hi]
        probs = eref[:, 0:hi] * weight
        low = probs.astype(BF)
        ds = (probs * (dref[:, 0:hi] - aref[h, :, 0:hi])).astype(BF)
        dk = dot(ds, qn[h, 0:hi, :]) * SCALE
        dv = dot(low, do[h, 0:hi, :])
        dqt[h, :, 0:hi] += dot(keys.astype(F32).T.astype(BF), ds)
        return dk, dv

    def backward_window(k, h):
        dk, dv = backward(window_keys(k, h)[0], h, RC, mw[k, h], ew.at[k, h], dw.at[k, h])
        ew[k, h, :, 0:HD] = dk
        ew[k, h, :, HD : 2 * HD] = dv

    def backward_prompt(j, h):
        dk, dv = backward(prompt_keys(j, h)[0], h, COLS, mp[j, h], ep.at[j, h], dp.at[j, h])
        ep[j, h, :, 0:HD] = dk
        ep[j, h, :, HD : 2 * HD] = dv
        for i in range(2):
            part = slice((2 * i + 1) * PROWS, (2 * i + 2) * PROWS)
            ys[2 * j + i, h, :, 0:HD] = dk[part].astype(BF)
            ys[2 * j + i, h, :, HD : 2 * HD] = dv[part].astype(BF)

    def return_first(h):
        backward_window(REACH, h)
        rets[REACH - 1, h] = ew[REACH, h, :, 0 : 2 * HD].astype(BF)
        back(REACH, h).start()

    loop(KH, return_first)

    def return_hop(k, h):
        back(k + 1, h).wait_recv()
        rets[k - 1, h] = (ew[k, h, :, 0 : 2 * HD] + retr[k, h].astype(F32)).astype(BF)
        back(k, h).start()

    def ring_sum(t):
        j = t // 2
        at = pl.multiple_of((t % 2) * (2 * PROWS), 2 * PROWS)
        return ep[j, :, pl.ds(at, PROWS), 0 : 2 * HD] + yr[t].astype(F32)

    def ring_first():
        scatter_y(NZ - 1).wait_recv()
        zs[NZ - 2] = ring_sum(NZ - 1).astype(BF)
        scatter_z(NZ - 1).start()

    def ring_hop(t):
        scatter_y(t).wait_recv()
        scatter_z(t + 1).wait_recv()
        zs[t - 1] = (ring_sum(t) + zr[t].astype(F32)).astype(BF)
        scatter_z(t).start()

    def ring_last():
        scatter_y(0).wait_recv()
        scatter_z(1).wait_recv()
        fin[...] = ring_sum(0) + zr[0].astype(F32)

    def return_step(n):
        s = 1 + n // KH
        h = n % KH
        backward_window(REACH + 1 - 2 * s, h)
        return_hop(REACH - s, h)
        backward_window(REACH - 2 * s, h)
        hop = NZ - 1 - (3 * (s - 2) + h)

        @pl.when((n == KH))
        def _():
            ring_first()

        @pl.when((n > KH) & (h < 3))
        def _():
            ring_hop(hop)

        j = NZ // 2 + 1 - 2 * s
        backward_prompt(j, h)
        backward_prompt(j - 1, h)

        @pl.when(h == KH - 1)
        def _():
            for i in range(4):
                scatter_y(2 * j + 1 - i).start()

    loop(KH * (REACH // 2), return_step)

    part = jnp.zeros((1, HD), F32)

    def query_back(raw, upstream):
        qhat, factor = rms(raw.astype(F32))
        u = upstream * g0
        inner = jnp.mean(u * qhat, axis=-1, keepdims=True)
        return factor * (u - qhat * inner), jnp.sum(upstream * qhat, axis=0, keepdims=True)

    for h in range(KH):
        tail = dqt[h, :, RC:COLS].T * SCALE
        for g in range(SH):
            head = h * SH + g
            cols = slice(head * HD, (head + 1) * HD)
            upstream = dqt[h, :, g * RROWS : (g + 1) * RROWS].T * SCALE
            out, more = query_back(qr[:, cols], upstream)
            dqr[:, cols] = out.astype(BF)
            part = part + more
            out, more = query_back(qp[:, cols], tail[g * PROWS : (g + 1) * PROWS])
            dqp[:, cols] = out.astype(BF)
            part = part + more
    red[0] = jnp.broadcast_to(part, (8, HD))

    def gain_copy(i):
        return pltpu.make_async_remote_copy(
            src_ref=red.at[i], dst_ref=redr.at[i], send_sem=rds.at[i], recv_sem=rdr.at[i],
            device_id=partners[i], device_id_type=MESH,
        )

    steps = len(partners)
    if steps:
        gain_copy(0).start()

    def gain_step(i):
        if i < steps:
            gain_copy(i).wait_recv()
            red[i + 1] = red[i] + redr[i]
            if i + 1 < steps:
                gain_copy(i + 1).start()

    done = 0
    for s in range(REACH // 2 + 1, REACH):
        for h in range(KH):
            return_hop(REACH - s, h)
            hop = NZ - 1 - (3 * (s - 2) + h)
            if h < 3 and hop > 0:
                ring_hop(hop)
            if h < 3 and hop == 0:
                ring_last()
            gain_step(done)
            done += 1
    while done < steps:
        gain_step(done)
        done += 1

    scales = [(total_rows * heads) ** (-0.5) for heads in (KH * SH, KH)]
    whole = red[steps][0:1, :]
    ngrad[0:1, :] = whole * scales[0]
    ngrad[1:2, :] = whole * (g0 / g1) * scales[1]

    def key_back(raw, upstream):
        khat, factor = rms(raw.astype(F32))
        u = upstream * g1
        inner = jnp.mean(u * khat, axis=-1, keepdims=True)
        return factor * (u - khat * inner)

    for h in range(KH):
        cols = slice(h * HD, (h + 1) * HD)
        vcols = slice((KH + h) * HD, (KH + h + 1) * HD)
        dkvp[:, cols] = key_back(kvp[:, cols], fin[h, :, 0:HD]).astype(BF)
        dkvp[:, vcols] = fin[h, :, HD : 2 * HD].astype(BF)
    for h in range(KH):
        cols = slice(h * HD, (h + 1) * HD)
        vcols = slice((KH + h) * HD, (KH + h + 1) * HD)
        back(1, h).wait_recv()
        own = ew[0, h, :, 0 : 2 * HD] + retr[0, h].astype(F32)
        dkvr[:, cols] = key_back(kvr[:, cols], own[:, 0:HD]).astype(BF)
        dkvr[:, vcols] = own[:, HD : 2 * HD].astype(BF)

    def sent(n):
        fwd(n // KH, n % KH).wait_send()
        back(n // KH + 1, n % KH).wait_send()

    loop(KH * REACH, sent)

    def ring_sent(t):
        gather_z(t).wait_send()
        scatter_z(t + 1).wait_send()
        gather_y(t).wait_send()
        scatter_y(t).wait_send()

    loop(NZ - 1, ring_sent)
    gather_y(NZ - 1).wait_send()
    scatter_y(NZ - 1).wait_send()
    for i in range(steps):
        gain_copy(i).wait_send()


def per_device(mesh_shape, qp, qr, kvp, kvr, gp, gr, gains, lens):
    bits = []
    for axis in ("resp", "prompt"):
        bit = 1
        while bit < mesh_shape[axis]:
            bits.append((axis, bit))
            bit *= 2
    total_rows = mesh_shape["prompt"] * mesh_shape["resp"] * (PROWS + RROWS)
    slots = max(1, len(bits))
    vmem = pl.BlockSpec(memory_space=pltpu.VMEM)
    dma = pltpu.SemaphoreType.DMA
    block = (KH, RROWS, 2 * HD)
    pblock = (KH, PROWS, 2 * HD)
    scratch = [
        pltpu.VMEM((REACH + 1,) + block, BF),
        pltpu.VMEM((NZ, 2) + pblock, BF),
        pltpu.VMEM((REACH,) + block, BF),
        pltpu.VMEM((REACH,) + block, BF),
        pltpu.VMEM((NZ - 1,) + pblock, BF),
        pltpu.VMEM((NZ - 1,) + pblock, BF),
        pltpu.VMEM((NZ,) + pblock, BF),
        pltpu.VMEM((NZ,) + pblock, BF),
        pltpu.VMEM(pblock, F32),
        pltpu.VMEM((KH, COLS, HD), BF),
        pltpu.VMEM((KH, HD, COLS), BF),
        pltpu.VMEM((KH, COLS, HD), BF),
        pltpu.VMEM((KH, HD, COLS), BF),
        pltpu.VMEM((KH, HD, COLS), F32),
        pltpu.VMEM((REACH + 1, KH, RROWS, RC), F32),
        pltpu.VMEM((REACH + 1, KH, RROWS, RC), F32),
        pltpu.VMEM((NZ // 2, KH, 4 * PROWS, COLS), F32),
        pltpu.VMEM((NZ // 2, KH, 4 * PROWS, COLS), F32),
        pltpu.VMEM((KH, 1, COLS), F32),
        pltpu.VMEM((KH, 1, COLS), F32),
        pltpu.VMEM((KH, 1, COLS), F32),
        pltpu.VMEM((REACH + 1, KH, 1, RC), F32),
        pltpu.VMEM((NZ // 2, KH, 1, COLS), F32),
        pltpu.VMEM((slots + 1, 8, HD), F32),
        pltpu.VMEM((slots, 8, HD), F32),
        dma((REACH, KH)), dma((REACH, KH)), dma((REACH, KH)), dma((REACH, KH)),
        dma((NZ - 1,)), dma((NZ - 1,)), dma((NZ,)), dma((NZ,)),
        dma((NZ - 1,)), dma((NZ - 1,)), dma((NZ,)), dma((NZ,)),
        dma((slots,)), dma((slots,)),
    ]
    width = qp.shape[2]
    kvwidth = kvp.shape[2]
    outs = pl.pallas_call(
        functools.partial(kernel, tuple(bits), total_rows),
        out_shape=(
            jax.ShapeDtypeStruct((PROWS, width), BF),
            jax.ShapeDtypeStruct((RROWS, width), BF),
            jax.ShapeDtypeStruct((PROWS, kvwidth), BF),
            jax.ShapeDtypeStruct((RROWS, kvwidth), BF),
            jax.ShapeDtypeStruct((2, HD), F32),
        ),
        in_specs=[vmem] * 7 + [pl.BlockSpec(memory_space=pltpu.SMEM)],
        out_specs=(vmem,) * 5,
        scratch_shapes=scratch,
        compiler_params=pltpu.CompilerParams(
            collective_id=0, has_side_effects=True, vmem_limit_bytes=62 * 1024 * 1024
        ),
    )(qp[0], qr[0], kvp[0], kvr[0], gp[0], gr[0], gains, lens)
    return outs[0][None], outs[1][None], outs[2][None], outs[3][None], outs[4]


def solution(mesh):
    rows = P("prompt", "resp", None)
    return jax.shard_map(
        functools.partial(per_device, dict(mesh.shape)),
        mesh=mesh,
        in_specs=(rows,) * 6 + (P(), P("prompt", None)),
        out_specs=(rows,) * 4 + (P(),),
        check_vma=False,
    )
```

time: 1000 us -> 187 us (0.19)
  the two profiles are of different devices: /device:TPU:1 before, /device:TPU:2 now
where the time goes in v1:
time: 187 us
  Pallas kernels  181 us (97%)
  local copies, waits for them, and re-layouts  5.4 us (3%)
    pallas_call x1, Pallas kernels, per_device(): pl.pallas_call(functools.partial(kernel, tuple(bits), total_rows), out_sh...  181 us
    unnamed x11, local copies, waits for them, and re-layouts  5.4 us

profile of v1, /device:TPU:2, one launch (start us, length us, event | category | flops | bytes accessed | tf_op | source)
XLA Modules:
  0.0 187.1 jit_solution(928991284167716793)
XLA Ops:
  0.6 181.0 %shard_map.119 = (bf16[32,2048]{1,0:T(8,128)(2,1)}, bf16[128,2048]{1,0:T(8,128)(2,1)}, bf16[32,1024]{1,0:T(8,128)(2,1)}, bf16[128,1024]{1,0:T(8,128)(2,1)}, f32[2,128]{1,0:T(2,128)}) custom-call(bf16[32,2048]{1,0:T(8,128)(2,1)} %bitcast.16, bf16[128,2048]{1,0:T(8,128)(2,1)} %bitcast.10, bf16[32,1024]{1,0:T(8,128)(2,1)} %bitcast.19, ...), custom_call_target="tpu_custom_call" | custom-call | tf_op jit(solution)/shard_map/pallas_call | solution.py:483
  181.7 1.6 copy.18
  183.2 0.0 copy-start.1
  183.2 0.0 copy-start
  183.2 1.9 %copy.19 = bf16[1,128,2048]{2,1,0:T(8,128)(2,1)} copy(bf16[1,128,2048]{2,1,0:T(8,128)(2,1)} %bitcast.12) | data formatting | bytes 1048576
  185.2 0.0 copy-done.1
  185.2 0.6 copy.20
  185.8 0.0 copy-done
  185.8 0.0 copy-start.2
  185.8 0.7 copy.21
  186.5 0.0 copy-done.2
  186.5 0.6 copy.22
Async XLA Ops:
  183.2 1.9 %copy-start.1 = (bf16[32,1024]{1,0:T(8,128)(2,1)S(1)}, bf16[32,1024]{1,0:T(8,128)(2,1)}, u32[]{:S(2)}) copy-start(bf16[32,1024]{1,0:T(8,128)(2,1)} %get-tuple-element.12) | copy-start | bytes 196612
  183.2 2.6 %copy-start = (bf16[128,1024]{1,0:T(8,128)(2,1)S(1)}, bf16[128,1024]{1,0:T(8,128)(2,1)}, u32[]{:S(2)}) copy-start(bf16[128,1024]{1,0:T(8,128)(2,1)} %get-tuple-element.13) | copy-start | bytes 786436
  185.8 0.7 copy-start.2

commit v2 on v1

--- a/solution.py
+++ b/solution.py
@@ -40,14 +40,14 @@
 
 
 def kernel(
-    bits,
+    rounds,
     total_rows,
     qp, qr, kvp, kvr, gp, gr, gains, lens,
     dqp, dqr, dkvp, dkvr, ngrad,
-    win, pg, retr, rets, zr, zs, yr, ys, fin,
+    win, pg, retr, rets, zr, zs, yr, ys, sider, sides, fin,
     qn, qt, do, dt, dqt, ew, dw, ep, dp,
     mref, lref, aref, mw, mp, red, redr,
-    fs, fr, bs, br, azs, azr, ays, ayr, rzs, rzr, rys, ryr, rds, rdr,
+    fs, fr, fxs, bs, br, bxs, azs, azr, ays, ayr, rzs, rzr, rys, ryr, rxs, rxr, rds, rdr,
 ):
     me = lax.axis_index("resp")
     pr = lax.axis_index("prompt")
@@ -55,17 +55,27 @@
     z = me % NZ
     nxt = (me + 1) % (2 * NZ)
     prv = (me + 2 * NZ - 1) % (2 * NZ)
-    znx = y * NZ + (z + 1) % NZ
-    zpv = y * NZ + (z + NZ - 1) % NZ
+    up1 = y * NZ + (z + 1) % NZ
+    up2 = y * NZ + (z + 2) % NZ
+    down1 = y * NZ + (z + NZ - 1) % NZ
+    down2 = y * NZ + (z + NZ - 2) % NZ
     yp = (me + NZ) % (2 * NZ)
 
+    def flipped(place, axis, bit):
+        if axis == "prompt":
+            return flip(place[0], bit), place[1]
+        return place[0], flip(place[1], bit)
+
     partners = []
-    for axis, bit in bits:
-        if axis == "resp":
-            partners.append((pr, flip(me, bit)))
-        else:
-            partners.append((flip(pr, bit), me))
-    friends = [(pr, nxt), (pr, prv), (pr, znx), (pr, zpv), (pr, yp)] + partners
+    for pair in rounds:
+        places = [flipped((pr, me), *pair[0])]
+        if len(pair) == 2:
+            other = flipped((pr, me), *pair[1])
+            places += [other, flipped(other, *pair[0])]
+        partners.append(places)
+    friends = [(pr, i) for i in (nxt, prv, up1, up2, down1, down2, yp)]
+    for places in partners:
+        friends += places
 
     barrier = pltpu.get_barrier_semaphore()
     for friend in friends:
@@ -80,23 +90,88 @@
             device_id=(pr, resp), device_id_type=MESH,
         )
 
+    def onward(h, ring, row):
+        return ring + (h // 2) * (row - ring)
+
     def fwd(k, h):
-        return remote(win.at[k, h], win.at[k + 1, h], fs.at[k, h], fr.at[k, h], nxt)
+        to = onward(h, nxt, up1)
+        return remote(win.at[k, h], win.at[k + 1, h], fs.at[k, h], fr.at[k, h], to)
+
+    def fwd_over(k, h):
+        return remote(win.at[k + 1, h], win.at[k + 1, h], fxs.at[k, h], fr.at[k, h], yp)
 
     def back(k, h):
-        return remote(rets.at[k - 1, h], retr.at[k - 1, h], bs.at[k - 1, h], br.at[k - 1, h], prv)
-
-    def gather_z(t):
-        return remote(pg.at[t, 0], pg.at[t + 1, 0], azs.at[t], azr.at[t], zpv)
-
-    def gather_y(t):
+        to = onward(h, prv, down1)
+        i = k - 1
+        return remote(rets.at[i, h], retr.at[i, h], bs.at[i, h], br.at[i, h], to)
+
+    def back_over(k, h):
+        i = k - 1
+        return remote(retr.at[i, h], retr.at[i, h], bxs.at[i, h], br.at[i, h], yp)
+
+    def fwd_sends(h):
+        return (h < KH // 2) | (me != 2 * NZ - 1)
+
+    def back_sends(h):
+        return (h < KH // 2) | (me != 0)
+
+    def fwd_start(k, h):
+        @pl.when(fwd_sends(h))
+        def _():
+            fwd(k, h).start()
+
+    def back_start(k, h):
+        @pl.when(back_sends(h))
+        def _():
+            back(k, h).start()
+
+    def fwd_arrived(k, h):
+        fwd(k, h).wait_recv()
+
+        @pl.when((h >= KH // 2) & (me == 0))
+        def _():
+            fwd_over(k, h).start()
+
+    def back_arrived(k, h):
+        back(k, h).wait_recv()
+
+        @pl.when((h >= KH // 2) & (me == 2 * NZ - 1))
+        def _():
+            back_over(k, h).start()
+
+    def returned(k, h):
+        keep = jnp.where((h >= KH // 2) & (me == 2 * NZ - 1), 0.0, 1.0)
+        return retr[k, h].astype(F32) * keep
+
+    def gather_two(m):
+        t = 2 * m
+        return remote(pg.at[t, 0], pg.at[t + 2, 0], azs.at[t], azr.at[t], down2)
+
+    def gather_one(m):
+        t = 2 * m
+        return remote(pg.at[t, 0], pg.at[t + 1, 0], azs.at[t + 1], azr.at[t + 1], down1)
+
+    def gather_y(m):
+        t = 2 * m
         return remote(pg.at[t, 0], pg.at[t, 1], ays.at[t], ayr.at[t], yp)
 
-    def scatter_z(t):
-        return remote(zs.at[t - 1], zr.at[t - 1], rzs.at[t - 1], rzr.at[t - 1], znx)
-
-    def scatter_y(t):
-        return remote(ys.at[t], yr.at[t], rys.at[t], ryr.at[t], yp)
+    def gather_side(m):
+        t = 2 * m
+        return remote(pg.at[t, 1], pg.at[t + 1, 1], ays.at[t + 1], ayr.at[t + 1], down1)
+
+    def scatter_one(m):
+        t = 2 * m
+        return remote(zs.at[t], zr.at[t], rzs.at[t], rzr.at[t], up1)
+
+    def scatter_two(m):
+        t = 2 * m - 1
+        return remote(zs.at[t], zr.at[t], rzs.at[t], rzr.at[t], up2)
+
+    def scatter_side(m):
+        return remote(sides.at[m], sider.at[m], rxs.at[m], rxr.at[m], up1)
+
+    def scatter_y(m):
+        return remote(ys.at[m], yr.at[m], rys.at[m], ryr.at[m], yp)
 
     for h in range(KH):
         cols = slice(h * HD, (h + 1) * HD)
@@ -109,10 +184,11 @@
         pg[0, 0, h, :, HD : 2 * HD] = kvp[:, vcols]
 
     pl.semaphore_wait(barrier, len(friends))
-    gather_z(0).start()
+    gather_two(0).start()
+    gather_one(0).start()
     gather_y(0).start()
     for h in range(KH):
-        fwd(0, h).start()
+        fwd_start(0, h)
 
     for h in range(KH):
         for g in range(SH):
@@ -213,22 +289,29 @@
     def forward_step(n):
         k = n // KH
         h = n % KH
-        fwd(k, h).wait_recv()
+        fwd_arrived(k, h)
 
         @pl.when(k < REACH - 1)
         def _():
-            fwd(k + 1, h).start()
-
-        t = 2 * k + 1 + h // 2
-
-        @pl.when((h % 2 == 0) & (t < NZ))
-        def _():
-            gather_z(t - 1).wait_recv()
-            gather_y(t).start()
-
-            @pl.when(t < NZ - 1)
+            fwd_start(k + 1, h)
+
+        @pl.when((n % 3 == 2) & (n < 3 * (NZ // 2)))
+        def _():
+            m = n // 3
+
+            @pl.when(m < NZ // 2 - 1)
             def _():
-                gather_z(t).start()
+                gather_two(m).wait_recv()
+
+                @pl.when(m < NZ // 2 - 2)
+                def _():
+                    gather_two(m + 1).start()
+
+                gather_one(m + 1).start()
+                gather_y(m + 1).start()
+
+            gather_y(m).wait_recv()
+            gather_side(m).start()
 
         forward_window(k + 1, h)
 
@@ -236,15 +319,21 @@
         def _():
             @pl.when(h == 0)
             def _():
-                gather_y(2 * k - 2).wait_recv()
-                gather_y(2 * k - 1).wait_recv()
+                gather_one(k - 1).wait_recv()
+                gather_side(k - 1).wait_recv()
 
             forward_prompt(k - 1, h)
 
+        @pl.when(k == REACH - 1)
+        def _():
+            @pl.when(h == 0)
+            def _():
+                gather_one(NZ // 2 - 1).wait_recv()
+                gather_side(NZ // 2 - 1).wait_recv()
+
+            forward_prompt(NZ // 2 - 1, h)
+
     loop(KH * REACH, forward_step)
-    gather_y(NZ - 2).wait_recv()
-    gather_y(NZ - 1).wait_recv()
-    loop(KH, lambda h: forward_prompt(NZ // 2 - 1, h))
 
     def finish(h):
         inverse = 1.0 / lref[h]
@@ -272,68 +361,88 @@
         dk, dv = backward(prompt_keys(j, h)[0], h, COLS, mp[j, h], ep.at[j, h], dp.at[j, h])
         ep[j, h, :, 0:HD] = dk
         ep[j, h, :, HD : 2 * HD] = dv
-        for i in range(2):
-            part = slice((2 * i + 1) * PROWS, (2 * i + 2) * PROWS)
-            ys[2 * j + i, h, :, 0:HD] = dk[part].astype(BF)
-            ys[2 * j + i, h, :, HD : 2 * HD] = dv[part].astype(BF)
+        sides[j, h, :, 0:HD] = dk[3 * PROWS :].astype(BF)
+        sides[j, h, :, HD : 2 * HD] = dv[3 * PROWS :].astype(BF)
 
     def return_first(h):
         backward_window(REACH, h)
         rets[REACH - 1, h] = ew[REACH, h, :, 0 : 2 * HD].astype(BF)
-        back(REACH, h).start()
+        back_start(REACH, h)
 
     loop(KH, return_first)
 
     def return_hop(k, h):
-        back(k + 1, h).wait_recv()
-        rets[k - 1, h] = (ew[k, h, :, 0 : 2 * HD] + retr[k, h].astype(F32)).astype(BF)
-        back(k, h).start()
-
-    def ring_sum(t):
-        j = t // 2
-        at = pl.multiple_of((t % 2) * (2 * PROWS), 2 * PROWS)
-        return ep[j, :, pl.ds(at, PROWS), 0 : 2 * HD] + yr[t].astype(F32)
+        back_arrived(k + 1, h)
+        rets[k - 1, h] = (ew[k, h, :, 0 : 2 * HD] + returned(k, h)).astype(BF)
+        back_start(k, h)
+
+    def prompt_part(j, quarter):
+        return ep[j, :, quarter * PROWS : (quarter + 1) * PROWS, 0 : 2 * HD]
+
+    def ring_odd(m):
+        zs[2 * m] = prompt_part(m, 2).astype(BF)
+        scatter_one(m).start()
+        scatter_side(m).start()
+
+    def ring_cross(m):
+        scatter_side(m).wait_recv()
+        ys[m] = (prompt_part(m, 1) + sider[m].astype(F32)).astype(BF)
+        scatter_y(m).start()
+
+    def ring_even(m):
+        scatter_y(m).wait_recv()
+        scatter_one(m).wait_recv()
+        return prompt_part(m, 0) + yr[m].astype(F32) + zr[2 * m].astype(F32)
 
     def ring_first():
-        scatter_y(NZ - 1).wait_recv()
-        zs[NZ - 2] = ring_sum(NZ - 1).astype(BF)
-        scatter_z(NZ - 1).start()
-
-    def ring_hop(t):
-        scatter_y(t).wait_recv()
-        scatter_z(t + 1).wait_recv()
-        zs[t - 1] = (ring_sum(t) + zr[t].astype(F32)).astype(BF)
-        scatter_z(t).start()
+        m = NZ // 2 - 1
+        zs[2 * m - 1] = ring_even(m).astype(BF)
+        scatter_two(m).start()
+
+    def ring_hop(m):
+        total = ring_even(m)
+        scatter_two(m + 1).wait_recv()
+        zs[2 * m - 1] = (total + zr[2 * m + 1].astype(F32)).astype(BF)
+        scatter_two(m).start()
 
     def ring_last():
-        scatter_y(0).wait_recv()
-        scatter_z(1).wait_recv()
-        fin[...] = ring_sum(0) + zr[0].astype(F32)
+        total = ring_even(0)
+        scatter_two(1).wait_recv()
+        fin[...] = total + zr[1].astype(F32)
 
     def return_step(n):
         s = 1 + n // KH
         h = n % KH
+
+        @pl.when(s > 1)
+        def _():
+            return_hop(REACH - s, h)
+
+        @pl.when((n >= 4) & (n % 2 == 0))
+        def _():
+            ring_cross(NZ // 2 - 1 - (n - 4) // 2)
+
+        @pl.when(n == 6)
+        def _():
+            ring_first()
+
+        @pl.when((n > 6) & (n % 3 == 0))
+        def _():
+            ring_hop(NZ // 2 - 1 - (n - 6) // 3)
+
         backward_window(REACH + 1 - 2 * s, h)
-        return_hop(REACH - s, h)
         backward_window(REACH - 2 * s, h)
-        hop = NZ - 1 - (3 * (s - 2) + h)
-
-        @pl.when((n == KH))
-        def _():
-            ring_first()
-
-        @pl.when((n > KH) & (h < 3))
-        def _():
-            ring_hop(hop)
-
-        j = NZ // 2 + 1 - 2 * s
-        backward_prompt(j, h)
-        backward_prompt(j - 1, h)
-
-        @pl.when(h == KH - 1)
-        def _():
-            for i in range(4):
-                scatter_y(2 * j + 1 - i).start()
+        j = NZ // 2 + 1 - 2 * s - h // 2
+        backward_prompt(j, 2 * (h % 2))
+        backward_prompt(j, 2 * (h % 2) + 1)
+
+        @pl.when(h % 2 == 1)
+        def _():
+            ring_odd(j)
+
+        @pl.when(s == 1)
+        def _():
+            return_hop(REACH - 1, h)
 
     loop(KH * (REACH // 2), return_step)
 
@@ -345,7 +454,8 @@
         inner = jnp.mean(u * qhat, axis=-1, keepdims=True)
         return factor * (u - qhat * inner), jnp.sum(upstream * qhat, axis=0, keepdims=True)
 
-    for h in range(KH):
+    def query_head(h):
+        total = jnp.zeros((1, HD), F32)
         tail = dqt[h, :, RC:COLS].T * SCALE
         for g in range(SH):
             head = h * SH + g
@@ -353,55 +463,62 @@
             upstream = dqt[h, :, g * RROWS : (g + 1) * RROWS].T * SCALE
             out, more = query_back(qr[:, cols], upstream)
             dqr[:, cols] = out.astype(BF)
-            part = part + more
+            total = total + more
             out, more = query_back(qp[:, cols], tail[g * PROWS : (g + 1) * PROWS])
             dqp[:, cols] = out.astype(BF)
-            part = part + more
-    red[0] = jnp.broadcast_to(part, (8, HD))
-
-    def gain_copy(i):
+            total = total + more
+        return total
+
+    def gain_copy(i, j):
         return pltpu.make_async_remote_copy(
-            src_ref=red.at[i], dst_ref=redr.at[i], send_sem=rds.at[i], recv_sem=rdr.at[i],
-            device_id=partners[i], device_id_type=MESH,
+            src_ref=red.at[i], dst_ref=redr.at[i, j], send_sem=rds.at[i, j], recv_sem=rdr.at[i, j],
+            device_id=partners[i][j], device_id_type=MESH,
         )
 
     steps = len(partners)
-    if steps:
-        gain_copy(0).start()
+
+    def gain_start(i):
+        if i < steps:
+            for j in range(len(partners[i])):
+                gain_copy(i, j).start()
 
     def gain_step(i):
         if i < steps:
-            gain_copy(i).wait_recv()
-            red[i + 1] = red[i] + redr[i]
-            if i + 1 < steps:
-                gain_copy(i + 1).start()
+            for j in range(len(partners[i])):
+                gain_copy(i, j).wait_recv()
+            total = red[i] + redr[i, 0]
+            if len(partners[i]) == 3:
+                total = total + (redr[i, 1] + redr[i, 2])
+            red[i + 1] = total
+            gain_start(i + 1)
 
     done = 0
     for s in range(REACH // 2 + 1, REACH):
         for h in range(KH):
             return_hop(REACH - s, h)
-            hop = NZ - 1 - (3 * (s - 2) + h)
-            if h < 3 and hop > 0:
-                ring_hop(hop)
-            if h < 3 and hop == 0:
+            n = KH * (s - 1) + h
+            if n % 2 == 0 and n < NZ + 4:
+                ring_cross(NZ // 2 - 1 - (n - 4) // 2)
+            if n % 3 == 0 and n < KH * REACH - 5:
+                ring_hop(NZ // 2 - 1 - (n - 6) // 3)
+            if n == KH * REACH - 5:
                 ring_last()
-            gain_step(done)
-            done += 1
-    while done < steps:
-        gain_step(done)
-        done += 1
-
-    scales = [(total_rows * heads) ** (-0.5) for heads in (KH * SH, KH)]
-    whole = red[steps][0:1, :]
-    ngrad[0:1, :] = whole * scales[0]
-    ngrad[1:2, :] = whole * (g0 / g1) * scales[1]
-
+            if s == REACH // 2 + 1:
+                part = part + query_head(h)
+                if h == KH - 1:
+                    red[0] = jnp.broadcast_to(part, (8, HD))
+                    gain_start(0)
+            elif h % 2 == 1:
+                gain_step(done)
+                done += 1
     def key_back(raw, upstream):
         khat, factor = rms(raw.astype(F32))
         u = upstream * g1
         inner = jnp.mean(u * khat, axis=-1, keepdims=True)
         return factor * (u - khat * inner)
 
+    for h in range(KH):
+        back_arrived(1, h)
     for h in range(KH):
         cols = slice(h * HD, (h + 1) * HD)
         vcols = slice((KH + h) * HD, (KH + h + 1) * HD)
@@ -410,39 +527,62 @@
     for h in range(KH):
         cols = slice(h * HD, (h + 1) * HD)
         vcols = slice((KH + h) * HD, (KH + h + 1) * HD)
-        back(1, h).wait_recv()
-        own = ew[0, h, :, 0 : 2 * HD] + retr[0, h].astype(F32)
+        own = ew[0, h, :, 0 : 2 * HD] + returned(0, h)
         dkvr[:, cols] = key_back(kvr[:, cols], own[:, 0:HD]).astype(BF)
         dkvr[:, vcols] = own[:, HD : 2 * HD].astype(BF)
 
+    while done < steps:
+        gain_step(done)
+        done += 1
+    scales = [(total_rows * heads) ** (-0.5) for heads in (KH * SH, KH)]
+    whole = red[steps][0:1, :]
+    ngrad[0:1, :] = whole * scales[0]
+    ngrad[1:2, :] = whole * (g0 / g1) * scales[1]
+
     def sent(n):
-        fwd(n // KH, n % KH).wait_send()
-        back(n // KH + 1, n % KH).wait_send()
+        k = n // KH
+        h = n % KH
+
+        @pl.when(fwd_sends(h))
+        def _():
+            fwd(k, h).wait_send()
+
+        @pl.when(back_sends(h))
+        def _():
+            back(k + 1, h).wait_send()
+
+        @pl.when((h >= KH // 2) & (me == 0))
+        def _():
+            fwd_over(k, h).wait_send()
+
+        @pl.when((h >= KH // 2) & (me == 2 * NZ - 1))
+        def _():
+            back_over(k + 1, h).wait_send()
 
     loop(KH * REACH, sent)
 
-    def ring_sent(t):
-        gather_z(t).wait_send()
-        scatter_z(t + 1).wait_send()
-        gather_y(t).wait_send()
-        scatter_y(t).wait_send()
-
-    loop(NZ - 1, ring_sent)
-    gather_y(NZ - 1).wait_send()
-    scatter_y(NZ - 1).wait_send()
+    def ring_sent(m):
+        gather_two(m).wait_send()
+        scatter_two(m + 1).wait_send()
+
+    loop(NZ // 2 - 1, ring_sent)
+
+    def half_sent(m):
+        for copy in (gather_one, gather_y, gather_side, scatter_one, scatter_y, scatter_side):
+            copy(m).wait_send()
+
+    loop(NZ // 2, half_sent)
     for i in range(steps):
-        gain_copy(i).wait_send()
+        for j in range(len(partners[i])):
+            gain_copy(i, j).wait_send()
 
 
 def per_device(mesh_shape, qp, qr, kvp, kvr, gp, gr, gains, lens):
-    bits = []
-    for axis in ("resp", "prompt"):
-        bit = 1
-        while bit < mesh_shape[axis]:
-            bits.append((axis, bit))
-            bit *= 2
+    bits = [("resp", 1 << i) for i in range((mesh_shape["resp"] - 1).bit_length())]
+    bits += [("prompt", 1 << i) for i in reversed(range((mesh_shape["prompt"] - 1).bit_length()))]
+    rounds = tuple(tuple(bits[i : i + 2]) for i in range(0, len(bits), 2))
     total_rows = mesh_shape["prompt"] * mesh_shape["resp"] * (PROWS + RROWS)
-    slots = max(1, len(bits))
+    slots = len(rounds)
     vmem = pl.BlockSpec(memory_space=pltpu.VMEM)
     dma = pltpu.SemaphoreType.DMA
     block = (KH, RROWS, 2 * HD)
@@ -454,8 +594,10 @@
         pltpu.VMEM((REACH,) + block, BF),
         pltpu.VMEM((NZ - 1,) + pblock, BF),
         pltpu.VMEM((NZ - 1,) + pblock, BF),
-        pltpu.VMEM((NZ,) + pblock, BF),
-        pltpu.VMEM((NZ,) + pblock, BF),
+        pltpu.VMEM((NZ // 2,) + pblock, BF),
+        pltpu.VMEM((NZ // 2,) + pblock, BF),
+        pltpu.VMEM((NZ // 2,) + pblock, BF),
+        pltpu.VMEM((NZ // 2,) + pblock, BF),
         pltpu.VMEM(pblock, F32),
         pltpu.VMEM((KH, COLS, HD), BF),
         pltpu.VMEM((KH, HD, COLS), BF),
@@ -472,16 +614,17 @@
         pltpu.VMEM((REACH + 1, KH, 1, RC), F32),
         pltpu.VMEM((NZ // 2, KH, 1, COLS), F32),
         pltpu.VMEM((slots + 1, 8, HD), F32),
-        pltpu.VMEM((slots, 8, HD), F32),
-        dma((REACH, KH)), dma((REACH, KH)), dma((REACH, KH)), dma((REACH, KH)),
-        dma((NZ - 1,)), dma((NZ - 1,)), dma((NZ,)), dma((NZ,)),
-        dma((NZ - 1,)), dma((NZ - 1,)), dma((NZ,)), dma((NZ,)),
-        dma((slots,)), dma((slots,)),
+        pltpu.VMEM((slots, 3, 8, HD), F32),
+        dma((REACH, KH)), dma((REACH, KH)), dma((REACH, KH)),
+        dma((REACH, KH)), dma((REACH, KH)), dma((REACH, KH)),
+        dma((NZ,)), dma((NZ,)), dma((NZ,)), dma((NZ,)),
+        dma((NZ,)), dma((NZ,)), dma((NZ // 2,)), dma((NZ // 2,)), dma((NZ // 2,)), dma((NZ // 2,)),
+        dma((slots, 3)), dma((slots, 3)),
     ]
     width = qp.shape[2]
     kvwidth = kvp.shape[2]
     outs = pl.pallas_call(
-        functools.partial(kernel, tuple(bits), total_rows),
+        functools.partial(kernel, rounds, total_rows),
         out_shape=(
             jax.ShapeDtypeStruct((PROWS, width), BF),
             jax.ShapeDtypeStruct((RROWS, width), BF),

time: 187 us -> 159 us (0.85)
  the two profiles are of different devices: /device:TPU:2 before, /device:TPU:1 now
where the time goes in v2:
time: 159 us; the launch traced here: 158 us
  Pallas kernels  152 us (96%)
  local copies, waits for them, and re-layouts  5.4 us (3%)
    pallas_call x1, Pallas kernels, per_device(): pl.pallas_call(functools.partial(kernel, rounds, total_rows), out_shape=(...  152 us
    unnamed x11, local copies, waits for them, and re-layouts  5.4 us

profile of v2, /device:TPU:1, one launch (start us, length us, event | category | flops | bytes accessed | tf_op | source)
XLA Modules:
  0.0 158.4 jit_solution(5161844261595189327)
XLA Ops:
  0.6 152.3 %shard_map.119 = (bf16[32,2048]{1,0:T(8,128)(2,1)}, bf16[128,2048]{1,0:T(8,128)(2,1)}, bf16[32,1024]{1,0:T(8,128)(2,1)}, bf16[128,1024]{1,0:T(8,128)(2,1)}, f32[2,128]{1,0:T(2,128)}) custom-call(bf16[32,2048]{1,0:T(8,128)(2,1)} %bitcast.16, bf16[128,2048]{1,0:T(8,128)(2,1)} %bitcast.10, bf16[32,1024]{1,0:T(8,128)(2,1)} %bitcast.19, ...), custom_call_target="tpu_custom_call" | custom-call | tf_op jit(solution)/shard_map/pallas_call | solution.py:626
  153.0 1.6 copy.18
  154.5 0.0 copy-start.1
  154.5 0.0 copy-start
  154.5 1.9 %copy.19 = bf16[1,128,2048]{2,1,0:T(8,128)(2,1)} copy(bf16[1,128,2048]{2,1,0:T(8,128)(2,1)} %bitcast.12) | data formatting | bytes 1048576
  156.5 0.0 copy-done.1
  156.5 0.6 copy.20
  157.1 0.0 copy-done
  157.1 0.0 copy-start.2
  157.1 0.7 copy.21
  157.8 0.0 copy-done.2
  157.8 0.6 copy.22
Async XLA Ops:
  154.5 1.9 %copy-start.1 = (bf16[32,1024]{1,0:T(8,128)(2,1)S(1)}, bf16[32,1024]{1,0:T(8,128)(2,1)}, u32[]{:S(2)}) copy-start(bf16[32,1024]{1,0:T(8,128)(2,1)} %get-tuple-element.12) | copy-start | bytes 196612
  154.5 2.6 %copy-start = (bf16[128,1024]{1,0:T(8,128)(2,1)S(1)}, bf16[128,1024]{1,0:T(8,128)(2,1)}, u32[]{:S(2)}) copy-start(bf16[128,1024]{1,0:T(8,128)(2,1)} %get-tuple-element.13) | copy-start | bytes 786436
  157.1 0.7 copy-start.2

commit v3 on v2

--- a/solution.py
+++ b/solution.py
@@ -44,10 +44,10 @@
     total_rows,
     qp, qr, kvp, kvr, gp, gr, gains, lens,
     dqp, dqr, dkvp, dkvr, ngrad,
-    win, pg, retr, rets, zr, zs, yr, ys, sider, sides, fin,
+    win, relay, pg, retr, rets, zr, zs, yr, ys, sider, sides, fin,
     qn, qt, do, dt, dqt, ew, dw, ep, dp,
     mref, lref, aref, mw, mp, red, redr,
-    fs, fr, fxs, bs, br, bxs, azs, azr, ays, ayr, rzs, rzr, rys, ryr, rxs, rxr, rds, rdr,
+    fs, fr, fxs, fxr, bs, br, bxs, bxr, azs, azr, ays, ayr, rzs, rzr, rys, ryr, rxs, rxr, rds, rdr,
 ):
     me = lax.axis_index("resp")
     pr = lax.axis_index("prompt")
@@ -67,12 +67,11 @@
         return place[0], flip(place[1], bit)
 
     partners = []
-    for pair in rounds:
-        places = [flipped((pr, me), *pair[0])]
-        if len(pair) == 2:
-            other = flipped((pr, me), *pair[1])
-            places += [other, flipped(other, *pair[0])]
-        partners.append(places)
+    for bits in rounds:
+        places = [(pr, me)]
+        for axis, bit in bits:
+            places += [flipped(place, axis, bit) for place in places]
+        partners.append(places[1:])
     friends = [(pr, i) for i in (nxt, prv, up1, up2, down1, down2, yp)]
     for places in partners:
         friends += places
@@ -90,58 +89,71 @@
             device_id=(pr, resp), device_id_type=MESH,
         )
 
-    def onward(h, ring, row):
-        return ring + (h // 2) * (row - ring)
+    first_device, last = me == 0, me == 2 * NZ - 1
+    leaves, enters = me == NZ - 1, me == NZ
+    half = KH // 2
 
     def fwd(k, h):
-        to = onward(h, nxt, up1)
-        return remote(win.at[k, h], win.at[k + 1, h], fs.at[k, h], fr.at[k, h], to)
+        return remote(win.at[k, h], win.at[k + 1, h], fs.at[k, h], fr.at[k, h], nxt)
+
+    def fwd_corner(k, h):
+        return remote(win.at[k, h], relay.at[k, h - half], fs.at[k, h], fxr.at[k, h], yp)
 
     def fwd_over(k, h):
-        return remote(win.at[k + 1, h], win.at[k + 1, h], fxs.at[k, h], fr.at[k, h], yp)
+        return remote(relay.at[k, h - half], win.at[k + 1, h], fxs.at[k, h], fr.at[k, h], up1)
 
     def back(k, h):
-        to = onward(h, prv, down1)
         i = k - 1
-        return remote(rets.at[i, h], retr.at[i, h], bs.at[i, h], br.at[i, h], to)
+        return remote(rets.at[i, h], retr.at[i, h], bs.at[i, h], br.at[i, h], prv)
+
+    def back_corner(k, h):
+        i = k - 1
+        return remote(rets.at[i, h], relay.at[i, h - half], bs.at[i, h], bxr.at[i, h], yp)
 
     def back_over(k, h):
         i = k - 1
-        return remote(retr.at[i, h], retr.at[i, h], bxs.at[i, h], br.at[i, h], yp)
-
-    def fwd_sends(h):
-        return (h < KH // 2) | (me != 2 * NZ - 1)
-
-    def back_sends(h):
-        return (h < KH // 2) | (me != 0)
+        return remote(relay.at[i, h - half], retr.at[i, h], bxs.at[i, h], br.at[i, h], down1)
 
     def fwd_start(k, h):
-        @pl.when(fwd_sends(h))
+        @pl.when((h >= half) & leaves)
+        def _():
+            fwd_corner(k, h).start()
+
+        @pl.when(((h < half) | (me != NZ - 1)) & (me != 2 * NZ - 1))
         def _():
             fwd(k, h).start()
 
     def back_start(k, h):
-        @pl.when(back_sends(h))
+        @pl.when((h >= half) & enters)
+        def _():
+            back_corner(k, h).start()
+
+        @pl.when(((h < half) | (me != NZ)) & (me != 0))
         def _():
             back(k, h).start()
 
     def fwd_arrived(k, h):
-        fwd(k, h).wait_recv()
-
-        @pl.when((h >= KH // 2) & (me == 0))
-        def _():
+        @pl.when((h >= half) & last)
+        def _():
+            fwd_corner(k, h).wait_recv()
             fwd_over(k, h).start()
 
+        @pl.when(me != 0)
+        def _():
+            fwd(k, h).wait_recv()
+
     def back_arrived(k, h):
-        back(k, h).wait_recv()
-
-        @pl.when((h >= KH // 2) & (me == 2 * NZ - 1))
-        def _():
+        @pl.when((h >= half) & first_device)
+        def _():
+            back_corner(k, h).wait_recv()
             back_over(k, h).start()
 
+        @pl.when(me != 2 * NZ - 1)
+        def _():
+            back(k, h).wait_recv()
+
     def returned(k, h):
-        keep = jnp.where((h >= KH // 2) & (me == 2 * NZ - 1), 0.0, 1.0)
-        return retr[k, h].astype(F32) * keep
+        return jnp.where(last, 0.0, retr[k, h].astype(F32))
 
     def gather_two(m):
         t = 2 * m
@@ -172,6 +184,14 @@
 
     def scatter_y(m):
         return remote(ys.at[m], yr.at[m], rys.at[m], ryr.at[m], yp)
+
+    @pl.when(first_device)
+    def _():
+        win[1:] = jnp.zeros((REACH, KH, RROWS, 2 * HD), BF)
+
+    @pl.when(last)
+    def _():
+        retr[...] = jnp.zeros((REACH, KH, RROWS, 2 * HD), BF)
 
     for h in range(KH):
         cols = slice(h * HD, (h + 1) * HD)
@@ -246,9 +266,9 @@
         keys, vals = window_keys(0, h)
         index = key_rows(0)
         allowed = (index >= first) & (index <= row_index)
-        start = jnp.full((1, RC), MASKED, F32)
+        lowest = jnp.full((1, RC), MASKED, F32)
         zero = jnp.zeros((1, RC), F32)
-        top = online(keys, vals, h, 0, RC, allowed, ew.at[0, h], dw.at[0, h], start, zero, zero)
+        top = online(keys, vals, h, 0, RC, allowed, ew.at[0, h], dw.at[0, h], lowest, zero, zero)
         mw[0, h] = top
         mref[h, :, RC:COLS] = jnp.full((1, PC), MASKED, F32)
         lref[h, :, RC:COLS] = jnp.zeros((1, PC), F32)
@@ -486,12 +506,16 @@
         if i < steps:
             for j in range(len(partners[i])):
                 gain_copy(i, j).wait_recv()
-            total = red[i] + redr[i, 0]
-            if len(partners[i]) == 3:
-                total = total + (redr[i, 1] + redr[i, 2])
-            red[i + 1] = total
+            parts = [red[i]] + [redr[i, j] for j in range(len(partners[i]))]
+            while len(parts) > 1:
+                parts = [parts[j] + parts[j + 1] for j in range(0, len(parts), 2)]
+            red[i + 1] = parts[0]
             gain_start(i + 1)
 
+    for h in range(KH):
+        part = part + query_head(h)
+    red[0] = jnp.broadcast_to(part, (8, HD))
+    gain_start(0)
     done = 0
     for s in range(REACH // 2 + 1, REACH):
         for h in range(KH):
@@ -503,12 +527,7 @@
                 ring_hop(NZ // 2 - 1 - (n - 6) // 3)
             if n == KH * REACH - 5:
                 ring_last()
-            if s == REACH // 2 + 1:
-                part = part + query_head(h)
-                if h == KH - 1:
-                    red[0] = jnp.broadcast_to(part, (8, HD))
-                    gain_start(0)
-            elif h % 2 == 1:
+            if (s, h) in ((REACH - 2, 0), (REACH - 1, 0), (REACH - 1, KH - 1)):
                 gain_step(done)
                 done += 1
     def key_back(raw, upstream):
@@ -543,19 +562,19 @@
         k = n // KH
         h = n % KH
 
-        @pl.when(fwd_sends(h))
+        @pl.when(me != 2 * NZ - 1)
         def _():
             fwd(k, h).wait_send()
 
-        @pl.when(back_sends(h))
+        @pl.when(me != 0)
         def _():
             back(k + 1, h).wait_send()
 
-        @pl.when((h >= KH // 2) & (me == 0))
+        @pl.when((h >= half) & last)
         def _():
             fwd_over(k, h).wait_send()
 
-        @pl.when((h >= KH // 2) & (me == 2 * NZ - 1))
+        @pl.when((h >= half) & first_device)
         def _():
             back_over(k + 1, h).wait_send()
 
@@ -577,10 +596,15 @@
             gain_copy(i, j).wait_send()
 
 
+def copy_out(*refs):
+    for source, target in zip(refs[:5], refs[5:]):
+        target[...] = source[...]
+
+
 def per_device(mesh_shape, qp, qr, kvp, kvr, gp, gr, gains, lens):
     bits = [("resp", 1 << i) for i in range((mesh_shape["resp"] - 1).bit_length())]
     bits += [("prompt", 1 << i) for i in reversed(range((mesh_shape["prompt"] - 1).bit_length()))]
-    rounds = tuple(tuple(bits[i : i + 2]) for i in range(0, len(bits), 2))
+    rounds = tuple(tuple(bits[i : i + 3]) for i in range(0, len(bits), 3))
     total_rows = mesh_shape["prompt"] * mesh_shape["resp"] * (PROWS + RROWS)
     slots = len(rounds)
     vmem = pl.BlockSpec(memory_space=pltpu.VMEM)
@@ -589,6 +613,7 @@
     pblock = (KH, PROWS, 2 * HD)
     scratch = [
         pltpu.VMEM((REACH + 1,) + block, BF),
+        pltpu.VMEM((REACH, KH // 2, RROWS, 2 * HD), BF),
         pltpu.VMEM((NZ, 2) + pblock, BF),
         pltpu.VMEM((REACH,) + block, BF),
         pltpu.VMEM((REACH,) + block, BF),
@@ -614,12 +639,12 @@
         pltpu.VMEM((REACH + 1, KH, 1, RC), F32),
         pltpu.VMEM((NZ // 2, KH, 1, COLS), F32),
         pltpu.VMEM((slots + 1, 8, HD), F32),
-        pltpu.VMEM((slots, 3, 8, HD), F32),
-        dma((REACH, KH)), dma((REACH, KH)), dma((REACH, KH)),
-        dma((REACH, KH)), dma((REACH, KH)), dma((REACH, KH)),
+        pltpu.VMEM((slots, 7, 8, HD), F32),
+        dma((REACH, KH)), dma((REACH, KH)), dma((REACH, KH)), dma((REACH, KH)),
+        dma((REACH, KH)), dma((REACH, KH)), dma((REACH, KH)), dma((REACH, KH)),
         dma((NZ,)), dma((NZ,)), dma((NZ,)), dma((NZ,)),
         dma((NZ,)), dma((NZ,)), dma((NZ // 2,)), dma((NZ // 2,)), dma((NZ // 2,)), dma((NZ // 2,)),
-        dma((slots, 3)), dma((slots, 3)),
+        dma((slots, 7)), dma((slots, 7)),
     ]
     width = qp.shape[2]
     kvwidth = kvp.shape[2]
@@ -639,6 +664,12 @@
             collective_id=0, has_side_effects=True, vmem_limit_bytes=62 * 1024 * 1024
         ),
     )(qp[0], qr[0], kvp[0], kvr[0], gp[0], gr[0], gains, lens)
+    outs = pl.pallas_call(
+        copy_out,
+        out_shape=tuple(jax.ShapeDtypeStruct(out.shape, out.dtype) for out in outs),
+        in_specs=[vmem] * 5,
+        out_specs=(vmem,) * 5,
+    )(*outs)
     return outs[0][None], outs[1][None], outs[2][None], outs[3][None], outs[4]
 
 

time: 159 us -> 157 us (0.987)
  local copies, waits for them, and re-layouts: 5.4 us -> 0 us
  Pallas kernels: 152 us -> 156 us
    unnamed x11 -> x0, local copies, waits for them, and re-layouts: 5.4 us -> none
    pallas_call x0 -> x1, Pallas kernels: none -> 2.11 us  [per_device(): pl.pallas_call(copy_out, out_shape=tuple((jax.ShapeDtypeStruct(out.shape,...]
where the time goes in v3:
time: 157 us; the launch traced here: 156 us
  Pallas kernels  156 us (99%)
    pallas_call x1, Pallas kernels, per_device(): pl.pallas_call(functools.partial(kernel, rounds, total_rows), out_shape=(...  154 us

profile of v3, /device:TPU:1, one launch (start us, length us, event | category | flops | bytes accessed | tf_op | source)
XLA Modules:
  0.0 156.4 jit_solution(7791105379592953229)
XLA Ops:
  0.6 153.7 %shard_map.119 = (bf16[32,2048]{1,0:T(8,128)(2,1)}, bf16[128,2048]{1,0:T(8,128)(2,1)}, bf16[32,1024]{1,0:T(8,128)(2,1)}, bf16[128,1024]{1,0:T(8,128)(2,1)}, f32[2,128]{1,0:T(2,128)}) custom-call(bf16[32,2048]{1,0:T(8,128)(2,1)} %bitcast.13, bf16[128,2048]{1,0:T(8,128)(2,1)} %bitcast.10, bf16[32,1024]{1,0:T(8,128)(2,1)} %bitcast.15, ...), custom_call_target="tpu_custom_call" | custom-call | tf_op jit(solution)/shard_map/pallas_call | solution.py:651
  154.3 2.1 %shard_map.120 = (bf16[32,2048]{1,0:T(8,128)(2,1)}, bf16[128,2048]{1,0:T(8,128)(2,1)}, bf16[32,1024]{1,0:T(8,128)(2,1)}, bf16[128,1024]{1,0:T(8,128)(2,1)}, f32[2,128]{1,0:T(2,128)}) custom-call(bf16[32,2048]{1,0:T(8,128)(2,1)} %get-tuple-element.15.refs_0_, bf16[128,2048]{1,0:T(8,128)(2,1)} %get-tuple-element.16.refs_1_, ...), custom_call_target="tpu_custom_call" | custom-call | tf_op jit(solution)/shard_map/pallas_call | solution.py:667

commit v4 on v3

--- a/solution.py
+++ b/solution.py
@@ -527,7 +527,7 @@
                 ring_hop(NZ // 2 - 1 - (n - 6) // 3)
             if n == KH * REACH - 5:
                 ring_last()
-            if (s, h) in ((REACH - 2, 0), (REACH - 1, 0), (REACH - 1, KH - 1)):
+            if (s, h) in ((REACH - 2, KH - 1), (REACH - 1, KH - 1)):
                 gain_step(done)
                 done += 1
     def key_back(raw, upstream):

time: 157 us -> 154 us (0.981)
  Pallas kernels: 156 us -> 153 us
    pallas_call x1, Pallas kernels: 154 us -> 151 us  [per_device(): pl.pallas_call(functools.partial(kernel, rounds, total_rows), out_shape=(...]
where the time goes in v4:
time: 154 us
  Pallas kernels  153 us (99%)
    pallas_call x1, Pallas kernels, per_device(): pl.pallas_call(functools.partial(kernel, rounds, total_rows), out_shape=(...  151 us

profile of v4, /device:TPU:1, one launch (start us, length us, event | category | flops | bytes accessed | tf_op | source)
XLA Modules:
  0.0 153.7 jit_solution(6482971498488580835)
XLA Ops:
  0.6 151.0 %shard_map.119 = (bf16[32,2048]{1,0:T(8,128)(2,1)}, bf16[128,2048]{1,0:T(8,128)(2,1)}, bf16[32,1024]{1,0:T(8,128)(2,1)}, bf16[128,1024]{1,0:T(8,128)(2,1)}, f32[2,128]{1,0:T(2,128)}) custom-call(bf16[32,2048]{1,0:T(8,128)(2,1)} %bitcast.13, bf16[128,2048]{1,0:T(8,128)(2,1)} %bitcast.10, bf16[32,1024]{1,0:T(8,128)(2,1)} %bitcast.15, ...), custom_call_target="tpu_custom_call" | custom-call | tf_op jit(solution)/shard_map/pallas_call | solution.py:651
  151.6 2.1 %shard_map.120 = (bf16[32,2048]{1,0:T(8,128)(2,1)}, bf16[128,2048]{1,0:T(8,128)(2,1)}, bf16[32,1024]{1,0:T(8,128)(2,1)}, bf16[128,1024]{1,0:T(8,128)(2,1)}, f32[2,128]{1,0:T(2,128)}) custom-call(bf16[32,2048]{1,0:T(8,128)(2,1)} %get-tuple-element.15.refs_0_, bf16[128,2048]{1,0:T(8,128)(2,1)} %get-tuple-element.16.refs_1_, ...), custom_call_target="tpu_custom_call" | custom-call | tf_op jit(solution)/shard_map/pallas_call | solution.py:667
